TPU v7x, 128 devices: a whole 4x4x4 slice. The times are simulated.
128 devices in a mesh: row: 16 (over z, y_hi, core), loop: 8 (over x, y_lo).
Axes of the slice: x: 4, y: 4 (y_hi: 2, y_lo: 2; y = y_hi * 2 + y_lo), z: 4, core: 2. Of those that a mesh axis runs over, the one named last changes fastest.
Arguments:
- student_image: bfloat16 [20480, 1024], P(('row', 'loop')), may hold values from -12 to 12
- student_text: bfloat16 [20480, 1024], P(('row', 'loop')), may hold values from -12 to 12
- teacher_image: bfloat16 [20480, 1024], P('row', 'loop'), may hold values from -12 to 12
- teacher_text: bfloat16 [20480, 1024], P('row', 'loop'), may hold values from -12 to 12
- student_scale: float32 [1], replicated, may hold values from 30 to 100
- teacher_scale: float32 [1], replicated, may hold values from 30 to 100
Outputs:
- loss: float32 [1], replicated
- grad_image: bfloat16 [20480, 1024], P(('row', 'loop'))
- grad_text: bfloat16 [20480, 1024], P(('row', 'loop'))
All inputs are finite; a program needn't handle non-finite values.
Results may differ from a plain program's by a relative error of at most 0.014.
The roundings to bfloat16 on the way count: a program that leaves them out, or rounds other values in their place, can miss the bound.
Values may be sent and summed in bfloat16 or wider, within the bound.
No kernel may reach another device: no remote copies, remote signals or barrier semaphores. Data moves between devices by JAX's collectives and lax.ppermute only.
A program may use at most 128 MiB of HBM per device.

v0:
```python
import functools
import math

import jax
import jax.numpy as jnp
from jax import lax
from jax.experimental import pallas as pl
from jax.experimental.pallas import tpu as pltpu
from jax.sharding import PartitionSpec as P

EPS = 1e-06
AXES = ("row", "loop")
SIZES = {"z": 4, "yh": 2, "core": 2, "x": 4, "yl": 2}
F32, BF16 = jnp.float32, jnp.bfloat16
LOG2E = math.log2(math.e)
LN2 = math.log(2.0)
LANES = 128
VMEM_LIMIT = 64 * 2**20 - 2**18
PAIRS = [(k, j) for k in range(4) for j in range(2)]
VMEM = pl.BlockSpec(memory_space=pltpu.VMEM)
SMEM = pl.BlockSpec(memory_space=pltpu.SMEM)
ANY = pl.BlockSpec(memory_space=pl.ANY)


def index_of(pos):
    index = 0
    for name, size in SIZES.items():
        index = index * size + pos[name] % size
    return index


def positions():
    found = [{}]
    for name, size in SIZES.items():
        found = [{**pos, name: i} for pos in found for i in range(size)]
    return found


def send(value, **step):
    perm = []
    for pos in positions():
        to = dict(pos)
        for name, by in step.items():
            to[name] = pos[name] + by
        perm.append((index_of(pos), index_of(to)))
    return lax.ppermute(value, AXES, perm=perm)


def swap_bit(value, axis, bit):
    perm = []
    for pos in positions():
        perm.append((index_of(pos), index_of({**pos, axis: pos[axis] ^ bit})))
    return lax.ppermute(value, AXES, perm=perm)


def params(**kw):
    return pltpu.CompilerParams(vmem_limit_bytes=VMEM_LIMIT, **kw)


def shape(dims, dtype):
    return jax.ShapeDtypeStruct(dims, dtype)


def norm_of(values):
    return jnp.sqrt(jnp.sum(values * values, axis=1, keepdims=True) + EPS)


def unit(codes):
    values = codes.astype(F32)
    return (values / norm_of(values)).astype(BF16)


def place(where_ref, k, j):
    return lax.rem(where_ref[0] + k, 4) * 2 + lax.rem(where_ref[1] + j, 2)


def own_kernel(si, ti, image):
    rows = si.shape[0]
    image[:rows, :] = unit(si[...])
    width = ti.shape[1]
    for l in range(8):
        image[rows:, l * width : (l + 1) * width] = ti[l * rows : (l + 1) * rows, :]


def own_image(si, ti):
    rows, code = si.shape
    return pl.pallas_call(
        own_kernel,
        out_shape=shape((2 * rows, code), BF16),
        in_specs=[VMEM] * 2,
        out_specs=VMEM,
        compiler_params=params(),
        name="own_image",
    )(si, ti)


def own_text_kernel(where, st, parts, text):
    rows = st.shape[0]
    text[:rows, :] = unit(st[...])
    values = jnp.concatenate([parts[place(where, k, j)] for k, j in PAIRS], axis=1)
    text[rows:, :] = unit(values)


def own_text(where, st, parts):
    rows, code = st.shape
    return pl.pallas_call(
        own_text_kernel,
        out_shape=shape((2 * rows, code), BF16),
        in_specs=[SMEM, VMEM, VMEM],
        out_specs=VMEM,
        compiler_params=params(),
        name="own_text",
    )(where, st, parts)


def tie(values, after):
    return lax.optimization_barrier((values, after))[0]


def ring_own(own, ring, pair):
    return send(own, **{ring: 1}), send(own, **{ring: -1}), send(own, **{pair: 1})


def ring_other(other, ring):
    return send(other, **{ring: 1}), send(other, **{ring: -1})


def ring_far(before, after_other, ring):
    return send(before, **{ring: 1}), send(after_other, **{ring: -1})


def in_order(own, first, second, third):
    before, after, other = first
    before_other, after_other = second
    far, far_other = third
    return [own, other, after, after_other, far, far_other, before, before_other]


def sum_of(refs):
    return sum(ref[...].astype(F32) for ref in refs)


def block_of(term, blocks, index):
    rows, code = term.shape
    return pl.BlockSpec((rows // blocks, code), lambda i: (index, 0))


EARLY = (4, 5, 3, 6)
LATE = (2, 7)


def early_sum_kernel(n, *refs):
    for m in range(len(EARLY)):
        refs[n * len(EARLY) + m][...] = sum_of(refs[n * m : n * (m + 1)]).astype(BF16)


def early_sum(terms):
    n = len(terms)
    rows, code = terms[0].shape
    out = pl.BlockSpec((rows // 8, code), lambda i: (0, 0))
    return pl.pallas_call(
        functools.partial(early_sum_kernel, n),
        grid=(1,),
        out_shape=(shape((rows // 8, code), BF16),) * len(EARLY),
        in_specs=[block_of(t, 8, block) for block in EARLY for t in terms],
        out_specs=(out,) * len(EARLY),
        compiler_params=params(),
        name="early_sum",
    )(*(terms * len(EARLY)))


def ring_add_kernel(n, *refs):
    ahead, behind = refs[-2:]
    ahead[...] = sum_of(refs[: n + 1]).astype(BF16)
    behind[...] = sum_of(refs[n + 1 : 2 * n + 2]).astype(BF16)


def ring_add(terms, to_next, to_prev):
    n = len(terms)
    rows, code = to_next.shape
    own = pl.BlockSpec((rows, code), lambda i: (0, 0))
    return pl.pallas_call(
        functools.partial(ring_add_kernel, n),
        grid=(1,),
        out_shape=(shape((rows, code), BF16),) * 2,
        in_specs=[block_of(t, 8, LATE[0]) for t in terms]
        + [own]
        + [block_of(t, 8, LATE[1]) for t in terms]
        + [own],
        out_specs=(own,) * 2,
        compiler_params=params(),
        name="ring_add",
    )(*terms, to_next, *terms, to_prev)


def pair_sum_kernel(*refs):
    refs[-1][...] = sum_of(refs[:-1]).astype(BF16)


def pair_sum(terms, near):
    rows, code = near[0].shape
    own = pl.BlockSpec((rows, code), lambda i: (0, 0))
    return pl.pallas_call(
        pair_sum_kernel,
        grid=(1,),
        out_shape=shape((rows, code), BF16),
        in_specs=[block_of(t, 8, 1) for t in terms] + [own] * len(near),
        out_specs=own,
        compiler_params=params(),
        name="pair_sum",
    )(*terms, *near)


def final_kernel(*refs):
    codes, out = refs[-2:]
    total = sum_of(refs[:-2])
    values = codes[...].astype(F32)
    norm = norm_of(values)
    units = values / norm
    inner = jnp.sum(total * units, axis=1, keepdims=True)
    out[...] = ((total - units * inner) / norm).astype(BF16)


def finish(terms, near, got, codes):
    own = pl.BlockSpec(codes.shape, lambda i: (0, 0))
    return pl.pallas_call(
        final_kernel,
        grid=(1,),
        out_shape=shape(codes.shape, BF16),
        in_specs=[own] * (len(terms) + len(near) + 2),
        out_specs=own,
        compiler_params=params(),
        name="finish",
    )(*terms, *near, got, codes)


def fetch_images(where, images, held, sem, rows):
    copies = []
    for n, (k, j) in enumerate(PAIRS):
        start = pl.multiple_of(place(where, k, j) * rows, rows)
        copies.append(
            pltpu.make_async_copy(
                images[n].at[pl.ds(0, rows), :], held.at[pl.ds(start, rows), :], sem.at[n]
            )
        )
    return copies


def fetch_texts(texts, held, sem, rows, part):
    return [
        pltpu.make_async_copy(
            texts[n].at[pl.ds(part * rows, rows), :], held.at[pl.ds(n * rows, rows), :], sem.at[n]
        )
        for n in range(16)
    ]


def wait_texts(copies, step, columns, rows):
    done = 0
    for at in range(16 * rows // columns):
        need = min(16, -(-(at + 1) * columns // rows))

        @pl.when(step == at)
        def _():
            for copy in copies[done:need]:
                copy.wait()

        done = need


ROW_TILE = 256
COLS = 512


def lanes_of(value):
    return [value[:, n * LANES : (n + 1) * LANES] for n in range(value.shape[1] // LANES)]


def student_kernel(where, scale, *refs):
    images, texts = refs[:8], refs[8:24]
    slog, mout, sout = refs[24:27]
    held, text, sem_image, sem_text = refs[27:]
    step = pl.program_id(0)
    rows = held.shape[0] // 8

    text_copies = fetch_texts(texts, text, sem_text, rows, 0)

    @pl.when(step == 0)
    def _():
        image_copies = fetch_images(where, images, held, sem_image, rows)
        for copy in image_copies + text_copies:
            copy.start()
        for copy in image_copies:
            copy.wait()
        mout[...] = jnp.full(mout.shape, -1e30, F32)
        sout[...] = jnp.zeros(sout.shape, F32)

    wait_texts(text_copies, step, COLS, rows)
    factor = scale[0] * LOG2E
    cols = text[pl.ds(pl.multiple_of(step * COLS, COLS), COLS), :]

    for r in range(held.shape[0] // ROW_TILE):
        at = pl.ds(r * ROW_TILE, ROW_TILE)
        s = factor * lax.dot_general(
            held[at, :], cols, (((1,), (1,)), ((), ())), preferred_element_type=F32
        )
        slog[at, :] = s
        old = mout[at, :]
        parts = lanes_of(s)
        top = functools.reduce(jnp.maximum, parts, old)
        total = sout[at, :] * jnp.exp2(old - top)
        for part in parts:
            total += jnp.exp2(part - top)
        mout[at, :] = top
        sout[at, :] = total


def student_logits(where, scale, images, texts):
    rows = images[0].shape[0] // 2 * 8
    code = images[0].shape[1]
    width = 8 * texts[0].shape[0]
    return pl.pallas_call(
        student_kernel,
        grid=(width // COLS,),
        out_shape=(
            shape((rows, width), F32),
            shape((rows, LANES), F32),
            shape((rows, LANES), F32),
        ),
        in_specs=[SMEM, SMEM] + [ANY] * 24,
        out_specs=(
            pl.BlockSpec((rows, COLS), lambda i: (0, i)),
            pl.BlockSpec((rows, LANES), lambda i: (0, 0)),
            pl.BlockSpec((rows, LANES), lambda i: (0, 0)),
        ),
        scratch_shapes=[
            pltpu.VMEM((rows, code), BF16),
            pltpu.VMEM((width, code), BF16),
            pltpu.SemaphoreType.DMA((8,)),
            pltpu.SemaphoreType.DMA((16,)),
        ],
        compiler_params=params(),
        cost_estimate=pl.CostEstimate(
            flops=2 * rows * width * code, bytes_accessed=4 * rows * width, transcendentals=0
        ),
        name="student_logits",
    )(where, scale, *images, *texts)


def teacher_images_kernel(*refs):
    images, held, raw, sem = refs[:8], *refs[8:]
    rows = raw.shape[1]
    copies = [
        pltpu.make_async_copy(images[n].at[pl.ds(rows, rows), :], raw.at[n], sem.at[n])
        for n in range(8)
    ]
    for copy in copies:
        copy.start()
    for copy in copies:
        copy.wait()

    def block(l, carry):
        at = pl.ds(pl.multiple_of(l * LANES, LANES), LANES)
        values = [raw[n, :, at].astype(F32) for n in range(8)]
        square = sum(v * v for v in values)
        norm = jnp.sqrt(jnp.sum(square, axis=1, keepdims=True) + EPS)
        to = pl.ds(pl.multiple_of(l * rows, rows), rows)
        for n in range(8):
            held[to, n * LANES : (n + 1) * LANES] = (values[n] / norm).astype(BF16)
        return carry

    lax.fori_loop(0, 8, block, 0)


def teacher_images(images):
    rows, code = images[0].shape
    return pl.pallas_call(
        teacher_images_kernel,
        out_shape=shape((4 * rows, code), BF16),
        in_specs=[ANY] * 8,
        out_specs=VMEM,
        scratch_shapes=[pltpu.VMEM((8, rows // 2, code), BF16), pltpu.SemaphoreType.DMA((8,))],
        compiler_params=params(),
        name="teacher_images",
    )(*images)


def teacher_kernel(scale, *refs):
    held, texts = refs[0], refs[1:17]
    slog, ms, ss = refs[17:20]
    tlog, stats = refs[20:22]
    text, mt, st, ct, sem_text = refs[22:]
    step = pl.program_id(0)
    rows = held.shape[0] // 8
    text_copies = fetch_texts(texts, text, sem_text, rows, 1)

    @pl.when(step == 0)
    def _():
        for copy in text_copies:
            copy.start()
        mt[...] = jnp.full(mt.shape, -1e30, F32)
        st[...] = jnp.zeros(st.shape, F32)
        ct[...] = jnp.zeros(ct.shape, F32)

    wait_texts(text_copies, step, COLS, rows)
    factor = scale[0] * LOG2E
    cols = text[pl.ds(pl.multiple_of(step * COLS, COLS), COLS), :]

    for r in range(held.shape[0] // ROW_TILE):
        at = pl.ds(r * ROW_TILE, ROW_TILE)
        t = factor * lax.dot_general(
            held[at, :], cols, (((1,), (1,)), ((), ())), preferred_element_type=F32
        )
        tlog[at, :] = t
        s_parts = lanes_of(slog[at, :])
        t_parts = lanes_of(t)
        old = mt[at, :]
        top = functools.reduce(jnp.maximum, t_parts, old)
        shrink = jnp.exp2(old - top)
        total = st[at, :] * shrink
        cross = ct[at, :] * shrink
        for a, b in zip(t_parts, s_parts):
            e = jnp.exp2(a - top)
            total += e
            cross += e * (a - b)
        mt[at, :] = top
        st[at, :] = total
        ct[at, :] = cross

    @pl.when(step == pl.num_programs(0) - 1)
    def _():
        smax = jnp.max(ms[...], axis=1, keepdims=True)
        ssum = jnp.sum(ss[...] * jnp.exp2(ms[...] - smax), axis=1, keepdims=True)
        tmax = jnp.max(mt[...], axis=1, keepdims=True)
        shrink = jnp.exp2(mt[...] - tmax)
        tsum = jnp.sum(st[...] * shrink, axis=1, keepdims=True)
        cross = jnp.sum(ct[...] * shrink, axis=1, keepdims=True)
        lane = lax.broadcasted_iota(jnp.int32, ms.shape, 1)
        packed = jnp.zeros(ms.shape, F32)
        for n, value in enumerate((smax, ssum, tmax, tsum, cross)):
            packed = jnp.where(lane == n, value, packed)
        for n in range(8):
            stats[n] = packed.T[:8, :]


def teacher_logits(scale, image, texts, slog, ms, ss):
    rows, width = slog.shape
    code = image.shape[1]
    whole = pl.BlockSpec((rows, LANES), lambda i: (0, 0))
    return pl.pallas_call(
        teacher_kernel,
        grid=(width // COLS,),
        out_shape=(shape((rows, width), F32), shape((8, 8, rows), F32)),
        in_specs=[SMEM, pl.BlockSpec((rows, code), lambda i: (0, 0))]
        + [ANY] * 16
        + [pl.BlockSpec((rows, COLS), lambda i: (0, i)), whole, whole],
        out_specs=(
            pl.BlockSpec((rows, COLS), lambda i: (0, i)),
            pl.BlockSpec((8, 8, rows), lambda i: (0, 0, 0)),
        ),
        scratch_shapes=[
            pltpu.VMEM((width, code), BF16),
            pltpu.VMEM((rows, LANES), F32),
            pltpu.VMEM((rows, LANES), F32),
            pltpu.VMEM((rows, LANES), F32),
            pltpu.SemaphoreType.DMA((16,)),
        ],
        compiler_params=params(),
        cost_estimate=pl.CostEstimate(
            flops=2 * rows * width * code, bytes_accessed=8 * rows * width, transcendentals=0
        ),
        name="teacher_logits",
    )(scale, image, *texts, slog, ms, ss)


def merge_stats(stats, lses, lset, loss):
    smax = jnp.max(stats[:, 0, :], axis=0, keepdims=True)
    ssum = jnp.sum(stats[:, 1, :] * jnp.exp2(stats[:, 0, :] - smax), axis=0, keepdims=True)
    tmax = jnp.max(stats[:, 2, :], axis=0, keepdims=True)
    shrink = jnp.exp2(stats[:, 2, :] - tmax)
    tsum = jnp.sum(stats[:, 3, :] * shrink, axis=0, keepdims=True)
    cross = jnp.sum(stats[:, 4, :] * shrink, axis=0, keepdims=True)
    lse_s = smax + jnp.log2(ssum)
    lse_t = tmax + jnp.log2(tsum)
    diverge = LN2 * (cross / tsum - lse_t + lse_s)
    loss[...] = jnp.full(loss.shape, jnp.sum(diverge), F32)
    rows = stats.shape[2]
    lses[...] = jnp.broadcast_to(lse_s, (LANES, rows)).T
    lset[...] = jnp.broadcast_to(lse_t, (LANES, rows)).T


GCOLS = 256


def grads_kernel(where, scale, *refs):
    images, texts = refs[:8], refs[8:24]
    slog, tlog, stats = refs[24:27]
    keep, away, dimg, *early, loss = refs[27:35]
    held, text, grad, acc, low, lses, lset, sem_image, sem_text, sem_out = refs[35:]
    step = pl.program_id(0)
    steps = pl.num_programs(0)
    rows = held.shape[0] // 8
    image_copies = fetch_images(where, images, held, sem_image, rows)
    text_copies = fetch_texts(texts, text, sem_text, rows, 0)

    @pl.when(step == 0)
    def _():
        for copy in text_copies[:2] + image_copies + text_copies[2:]:
            copy.start()
        acc[...] = jnp.zeros(acc.shape, F32)
        merge_stats(stats, lses, lset, loss)
        for copy in image_copies:
            copy.wait()

    wait_texts(text_copies, step, GCOLS, rows)
    cols = text[pl.ds(pl.multiple_of(step * GCOLS, GCOLS), GCOLS), :]

    for r in range(held.shape[0] // ROW_TILE):
        at = pl.ds(r * ROW_TILE, ROW_TILE)
        ls, lt = lses[at, :], lset[at, :]
        parts = []
        for a, b in zip(lanes_of(slog[at, :]), lanes_of(tlog[at, :])):
            parts.append((scale[0] * (jnp.exp2(a - ls) - jnp.exp2(b - lt))).astype(BF16))
        g = jnp.concatenate(parts, axis=1)
        grad[at, :] = g
        acc[at, :] += jnp.dot(g, cols, preferred_element_type=F32)

    term = lax.dot_general(
        grad[...], held[...], (((0,), (0,)), ((), ())), preferred_element_type=F32
    ).astype(BF16)

    @pl.when(step < steps // 2)
    def _():
        keep[...] = term

    @pl.when(step >= steps // 2)
    def _():
        away[...] = term

    @pl.when(step == steps - 1)
    def _():
        low[...] = acc[...].astype(BF16)
        copies = []
        for n, (k, j) in enumerate(PAIRS):
            start = pl.multiple_of(place(where, k, j) * rows, rows)
            target = dimg.at[pl.ds(n * rows, rows), :]
            if n in EARLY:
                target = early[EARLY.index(n)]
            copies.append(
                pltpu.make_async_copy(low.at[pl.ds(start, rows), :], target, sem_out.at[n])
            )
        for copy in copies:
            copy.start()
        for copy in copies:
            copy.wait()


def grads(where, scale, images, texts, slog, tlog, stats):
    rows, width = slog.shape
    code = images[0].shape[1]
    own = rows // 8
    steps = width // GCOLS
    half = steps // 2
    column = pl.BlockSpec((rows, GCOLS), lambda i: (0, i))
    return pl.pallas_call(
        grads_kernel,
        grid=(steps,),
        out_shape=(
            shape((width // 2, code), BF16),
            shape((width // 2, code), BF16),
            shape((rows, code), BF16),
            *[shape((own, code), BF16)] * len(EARLY),
            shape((8, LANES), F32),
        ),
        in_specs=[SMEM, SMEM]
        + [ANY] * 24
        + [column, column, pl.BlockSpec(stats.shape, lambda i: (0, 0, 0))],
        out_specs=(
            pl.BlockSpec((GCOLS, code), lambda i: (jnp.minimum(i, half - 1), 0)),
            pl.BlockSpec((GCOLS, code), lambda i: (jnp.maximum(i - half, 0), 0)),
            *[ANY] * (1 + len(EARLY)),
            pl.BlockSpec((8, LANES), lambda i: (0, 0)),
        ),
        scratch_shapes=[
            pltpu.VMEM((rows, code), BF16),
            pltpu.VMEM((width, code), BF16),
            pltpu.VMEM((rows, GCOLS), BF16),
            pltpu.VMEM((rows, code), F32),
            pltpu.VMEM((rows, code), BF16),
            pltpu.VMEM((rows, LANES), F32),
            pltpu.VMEM((rows, LANES), F32),
            pltpu.SemaphoreType.DMA((8,)),
            pltpu.SemaphoreType.DMA((16,)),
            pltpu.SemaphoreType.DMA((8,)),
        ],
        compiler_params=params(),
        cost_estimate=pl.CostEstimate(
            flops=4 * rows * width * code, bytes_accessed=8 * rows * width, transcendentals=0
        ),
        name="grads",
    )(where, scale, *images, *texts, slog, tlog, stats)


def on_device(
    student_image, student_text, teacher_image, teacher_text, student_scale, teacher_scale
):
    rows = student_image.shape[0]
    loop = lax.axis_index("loop")
    where = jnp.stack([loop // 2, loop % 2]).astype(jnp.int32)

    parts = lax.all_to_all(
        teacher_text.reshape(8, rows, -1), "loop", split_axis=0, concat_axis=0
    )
    image_own = tie(own_image(student_image, teacher_image), parts)
    x_first = ring_own(image_own, "x", "yl")
    text_own = own_text(where, student_text, parts)
    z_first = ring_own(text_own, "z", "yh")
    x_second = ring_other(tie(x_first[2], x_first), "x")
    z_second = ring_other(tie(z_first[2], (x_first, z_first)), "z")
    x_third = ring_far(*tie((x_first[0], x_second[1]), (x_second, z_first)), "x")
    z_third = ring_far(*tie((z_first[0], z_second[1]), (x_second, z_second)), "z")
    images = in_order(image_own, x_first, x_second, x_third)
    timg = teacher_images(images)
    mine = in_order(text_own, z_first, z_second, tie(z_third, timg))
    texts = mine + [send(v, core=1) for v in mine]

    slog, ms, ss = student_logits(where, student_scale, images, texts)
    tlog, stats = teacher_logits(teacher_scale, timg, texts, slog, ms, ss)
    stats = lax.all_to_all(stats, "loop", split_axis=0, concat_axis=0)
    keep, away, dimg, *early, total = grads(
        where, student_scale, images, texts, slog, tlog, stats
    )
    got = send(away, core=1)

    def scatter(terms, early, ring):
        two, two_other, one_pair, three_own = early
        to_next = send(two, **{ring: 1})
        to_prev = send(two_other, **{ring: -1})
        pair_near = [send(one_pair, **{ring: 1})]
        own_near = [send(three_own, **{ring: -1})]
        ahead, behind = ring_add(terms, to_next, to_prev)
        own_near.append(send(ahead, **{ring: 1}))
        pair_near.append(send(behind, **{ring: -1}))
        return own_near, pair_near

    terms = (keep, got)
    x_own, x_pair = scatter((dimg,), early, "x")
    z_own, z_pair = scatter(terms, early_sum(terms), "z")
    for axis in ("core", "yh"):
        total = total + swap_bit(total, axis, 1)
    x_pair = tie(x_pair, total)
    x_got = send(pair_sum((dimg,), x_pair), yl=1)
    z_got = send(pair_sum(terms, z_pair), yh=1)
    total = tie(total, (z_own, z_pair))
    for bit in (1, 2):
        total = total + swap_bit(total, "z", bit)
    loss = (total[0, 0] / (rows * 128)).reshape(1)
    z_got = tie(z_got, total)
    return (
        loss,
        finish((dimg,), x_own, x_got, student_image),
        finish(terms, z_own, z_got, student_text),
    )


def solution(mesh):
    return jax.shard_map(
        on_device,
        mesh=mesh,
        in_specs=(
            P(("row", "loop"), None),
            P(("row", "loop"), None),
            P("row", "loop"),
            P("row", "loop"),
            P(),
            P(),
        ),
        out_specs=(P(), P(("row", "loop"), None), P(("row", "loop"), None)),
        check_vma=False,
    )
```

profile of v0, /device:TPU:0, one launch (start us, length us, event | category | flops | bytes accessed | tf_op | source)
XLA Modules:
  0.0 214.4 jit_solution(14535130539167758560)
XLA Ops:
  0.6 5.4 %all-to-all-start = ((bf16[8,160,128]{2,1,0:T(8,128)(2,1)}), bf16[8,160,128]{2,1,0:T(8,128)(2,1)}, u32[]{:S(2)}, u32[]{:S(2)}) async-start(bf16[8,160,128]{2,1,0:T(8,128)(2,1)} %bitcast.4), calls=%async_computation | async-start | bytes 655360 | tf_op jit(solution)/shard_map/all_to_all | solution.py:611
  6.0 2.2 %own_image.1.refs_0_ = bf16[320,1024]{1,0:T(8,128)(2,1)} custom-call(bf16[160,1024]{1,0:T(8,128)(2,1)} %refs_4_.1, bf16[1280,128]{1,0:T(8,128)(2,1)} %ti.1), custom_call_target="tpu_custom_call" | custom-call | tf_op jit(solution)/shard_map/own_image/pallas_call | solution.py:87
  8.2 5.6 %all-to-all-done.parts = bf16[8,160,128]{2,1,0:T(8,128)(2,1)} async-done(((bf16[8,160,128]{2,1,0:T(8,128)(2,1)}), bf16[8,160,128]{2,1,0:T(8,128)(2,1)}, u32[]{:S(2)}, u32[]{:S(2)}) %all-to-all-start) | async-done | bytes 327712 | tf_op jit(solution)/shard_map/all_to_all | solution.py:611
  14.1 2.9 %collective-permute-start.1 = (bf16[320,1024]{1,0:T(8,128)(2,1)}, bf16[320,1024]{1,0:T(8,128)(2,1)}, u32[]{:S(2)}, u32[]{:S(2)}) collective-permute-start(bf16[320,1024]{1,0:T(8,128)(2,1)} %own_image.1.refs_0_), channel_id=1, source_target_pairs={{0,6},{1,7},{2,0},{3,1},{4,2},{5,3},{6,4},{7,5},{8,14},{9,15},{10,... | collective-permute-start | bytes 1966088 | tf_op jit(solution)/shard_map/ppermute | solution.py:46
  17.0 1.2 collective-permute-start
  18.9 2.2 %own_text.1.refs_8_.refs_1_ = bf16[320,1024]{1,0:T(8,128)(2,1)} custom-call(s32[2]{0:T(128)} %pad_add_fusion.where, bf16[160,1024]{1,0:T(8,128)(2,1)} %refs_5_.1, bf16[8,160,128]{2,1,0:T(8,128)(2,1)} %all-to-all-done.parts), custom_call_target="tpu_custom_call" | custom-call | tf_op jit(solution)/shard_map/own_text/pallas_call | solution.py:106
  21.1 2.9 %collective-permute-start.7 = (bf16[320,1024]{1,0:T(8,128)(2,1)}, bf16[320,1024]{1,0:T(8,128)(2,1)}, u32[]{:S(2)}, u32[]{:S(2)}) collective-permute-start(bf16[320,1024]{1,0:T(8,128)(2,1)} %own_text.1.refs_8_.refs_1_), channel_id=1, source_target_pairs={{0,16},{1,17},{2,18},{3,19},{4,20},{5,21},{6,22},{7,23},{8,24},{9,... | collective-permute-start | bytes 1966088 | tf_op jit(solution)/shard_map/ppermute | solution.py:46
  24.0 4.0 %collective-permute-start.6 = (bf16[320,1024]{1,0:T(8,128)(2,1)}, bf16[320,1024]{1,0:T(8,128)(2,1)}, u32[]{:S(2)}, u32[]{:S(2)}) collective-permute-start(bf16[320,1024]{1,0:T(8,128)(2,1)} %own_text.1.refs_8_.refs_1_), channel_id=1, source_target_pairs={{0,96},{1,97},{2,98},{3,99},{4,100},{5,101},{6,102},{7,103},{8,104... | collective-permute-start | bytes 1966088 | tf_op jit(solution)/shard_map/ppermute | solution.py:46
  28.0 2.0 collective-permute-done.2.refs_6_
  30.0 1.9 collective-permute-start.5
  31.9 3.1 %collective-permute-done.refs_1_ = bf16[320,1024]{1,0:T(8,128)(2,1)} collective-permute-done((bf16[320,1024]{1,0:T(8,128)(2,1)}, bf16[320,1024]{1,0:T(8,128)(2,1)}, u32[]{:S(2)}, u32[]{:S(2)}) %collective-permute-start) | collective-permute-done | bytes 655392 | tf_op jit(solution)/shard_map/ppermute | solution.py:46
  35.0 3.2 %collective-permute-start.3 = (bf16[320,1024]{1,0:T(8,128)(2,1)}, bf16[320,1024]{1,0:T(8,128)(2,1)S(1)}, u32[]{:S(2)}, u32[]{:S(2)}) collective-permute-start(bf16[320,1024]{1,0:T(8,128)(2,1)} %collective-permute-done.refs_1_), channel_id=1, source_target_pairs={{0,6},{1,7},{2,0},{3,1},{4,2},{5,3},{6,4},{7,5},{8,14},{9,15},{10,... | collective-permute-start | bytes 1966088 | tf_op jit(solution)/shard_map/ppermute | solution.py:46
  38.2 9.9 %collective-permute-done.7.refs_9_.refs_2_ = bf16[320,1024]{1,0:T(8,128)(2,1)} collective-permute-done((bf16[320,1024]{1,0:T(8,128)(2,1)}, bf16[320,1024]{1,0:T(8,128)(2,1)}, u32[]{:S(2)}, u32[]{:S(2)}) %collective-permute-start.7) | collective-permute-done | bytes 655392 | tf_op jit(solution)/shard_map/ppermute | solution.py:46
  48.2 1.9 collective-permute-start.11
  50.1 2.2 %collective-permute-start.10 = (bf16[320,1024]{1,0:T(8,128)(2,1)}, bf16[320,1024]{1,0:T(8,128)(2,1)}, u32[]{:S(2)}, u32[]{:S(2)}) collective-permute-start(bf16[320,1024]{1,0:T(8,128)(2,1)} %collective-permute-done.7.refs_9_.refs_2_), channel_id=1, source_target_pairs={{0,96},{1,97},{2,98},{3,99},{4,100},{5,101},{6,102},{7,103},{8,104... | collective-permute-start | bytes 1966088 | tf_op jit(solution)/shard_map/ppermute | solution.py:46
  53.1 2.5 %collective-permute-start.9 = (bf16[320,1024]{1,0:T(8,128)(2,1)S(1)}, bf16[320,1024]{1,0:T(8,128)(2,1)S(1)}, u32[]{:S(2)}, u32[]{:S(2)}) collective-permute-start(bf16[320,1024]{1,0:T(8,128)(2,1)S(1)} %collective-permute-done.3.refs_3_), channel_id=1, source_target_pairs={{0,6},{1,7},{2,0},{3,1},{4,2},{5,3},{6,4},{7,5},{8,14},{9,15},{10,... | collective-permute-start | bytes 1966088 | tf_op jit(solution)/shard_map/ppermute | solution.py:46
  55.6 9.0 %collective-permute-done.11.refs_15_.refs_8_ = bf16[320,1024]{1,0:T(8,128)(2,1)} collective-permute-done((bf16[320,1024]{1,0:T(8,128)(2,1)}, bf16[320,1024]{1,0:T(8,128)(2,1)}, u32[]{:S(2)}, u32[]{:S(2)}) %collective-permute-start.11) | collective-permute-done | bytes 655392 | tf_op jit(solution)/shard_map/ppermute | solution.py:46
  64.6 1.3 collective-permute-start.12
  65.9 2.0 collective-permute-start.13
  70.0 4.8 %teacher_images.1.refs_0_ = bf16[1280,1024]{1,0:T(8,128)(2,1)} custom-call(bf16[320,1024]{1,0:T(8,128)(2,1)} %own_image.1.refs_0_, bf16[320,1024]{1,0:T(8,128)(2,1)} %collective-permute-done.refs_1_, bf16[320,1024]{1,0:T(8,128)(2,1)} %collective-permute-done.1.refs_2_, bf16[320,1024]{1,0:T(8,128)(2,1)} %copy-done, bf16[320,1024]{1,0:T(8,128)(2,1)} %copy-done.1, ...), custom_call_target="tpu_custom_call" | custom-call | tf_op jit(solution)/shard_map/teacher_images/pallas_call | solution.py:377
  74.8 4.4 %collective-permute-done.12.refs_12_.refs_5_ = bf16[320,1024]{1,0:T(8,128)(2,1)} collective-permute-done((bf16[320,1024]{1,0:T(8,128)(2,1)}, bf16[320,1024]{1,0:T(8,128)(2,1)}, u32[]{:S(2)}, u32[]{:S(2)}) %collective-permute-start.12) | collective-permute-done | bytes 655392 | tf_op jit(solution)/shard_map/ppermute | solution.py:46
  82.7 0.9 collective-permute-done.17.refs_19_.refs_12_
  83.6 0.9 collective-permute-done.18.refs_20_.refs_13_
  85.5 15.4 %student_logits.1 = (f32[1280,2560]{1,0:T(8,128)}, f32[1280,128]{1,0:T(8,128)}, f32[1280,128]{1,0:T(8,128)}) custom-call(s32[2]{0:T(128)} %pad_add_fusion.where, f32[1]{0:T(128)S(6)} %copy.9.scale, bf16[320,1024]{1,0:T(8,128)(2,1)} %own_image.1.refs_0_, bf16[320,1024]{1,0:T(8,128)(2,1)} %collective-permute-done.refs_1_, ...), custom_call_target="tpu_custom_call" | custom-call | flops 6710886400 | bytes 13107200 | tf_op jit(solution)/shard_map/student_logits/pallas_call | solution.py:322
  100.9 19.0 %teacher_logits.1 = (f32[1280,2560]{1,0:T(8,128)}, f32[8,8,1280]{2,1,0:T(8,128)}) custom-call(f32[1]{0:T(128)S(6)} %copy.10.scale, bf16[1280,1024]{1,0:T(8,128)(2,1)} %teacher_images.1.refs_0_, bf16[320,1024]{1,0:T(8,128)(2,1)} %own_text.1.refs_8_.refs_1_, bf16[320,1024]{1,0:T(8,128)(2,1)} %collective-permute-done.7.refs_9_.refs_2_, ...), custom_call_target="tpu_custom_call" | custom-call | flops 6710886400 | bytes 26214400 | tf_op jit(solution)/shard_map/teacher_logits/pallas_call | solution.py:450
  119.9 12.8 %all_to_all.10.refs_26_ = f32[8,8,1280]{2,1,0:T(8,128)} all-to-all(f32[8,8,1280]{2,1,0:T(8,128)} %get-tuple-element.50), channel_id=1, replica_groups=mesh['row'=16,'loop'=8] {'loop'}, dimensions={0} | all-to-all | bytes 655360 | tf_op jit(solution)/shard_map/all_to_all | solution.py:629
  132.7 26.0 %grads.1 = (bf16[1280,1024]{1,0:T(8,128)(2,1)}, bf16[1280,1024]{1,0:T(8,128)(2,1)}, bf16[1280,1024]{1,0:T(8,128)(2,1)}, bf16[160,1024]{1,0:T(8,128)(2,1)}, bf16[...) custom-call(s32[2]{0:T(128)} %pad_add_fusion.where, ...), custom_call_target="tpu_custom_call" | custom-call | flops 13421772800 | bytes 26214400 | tf_op jit(solution)/shard_map/grads/pallas_call | solution.py:565
  159.5 2.7 %collective-permute-start.35 = (bf16[160,1024]{1,0:T(8,128)(2,1)}, bf16[160,1024]{1,0:T(8,128)(2,1)}, u32[]{:S(2)}, u32[]{:S(2)}) collective-permute-start(bf16[160,1024]{1,0:T(8,128)(2,1)} %get-tuple-element.64), channel_id=1, source_target_pairs={{0,6},{1,7},{2,0},{3,1},{4,2},{5,3},{6,4},{7,5},{8,14},{9,15},{10,... | collective-permute-start | bytes 983048 | tf_op jit(solution)/shard_map/ppermute | solution.py:46
  162.2 1.9 collective-permute-done.24.refs_1_.refs_3_.refs_5_.refs_7_.refs_4_
  164.1 2.8 %early_sum.1 = (bf16[160,1024]{1,0:T(8,128)(2,1)}, bf16[160,1024]{1,0:T(8,128)(2,1)}, bf16[160,1024]{1,0:T(8,128)(2,1)}, bf16[160,1024]{1,0:T(8,128)(2,1)}) custom-call(bf16[1280,1024]{1,0:T(8,128)(2,1)} %get-tuple-element.52.refs_0_.refs_2_.refs_4_.refs_6_.refs_3_, bf16[1280,1024]{1,0:T(8,128)(2,1)} %collective-permute-done.24.refs_1_.refs_3_.refs_5_.refs_7_.refs_4_, ...), custom_call_target="tpu_custom_call" | custom-call | tf_op jit(solution)/shard_map/early_sum/pallas_call | solution.py:161
  166.9 3.2 %collective-permute-start.27 = (bf16[160,1024]{1,0:T(8,128)(2,1)}, bf16[160,1024]{1,0:T(8,128)(2,1)}, u32[]{:S(2)}, u32[]{:S(2)}) collective-permute-start(bf16[160,1024]{1,0:T(8,128)(2,1)} %get-tuple-element.56), channel_id=1, source_target_pairs={{0,96},{1,97},{2,98},{3,99},{4,100},{5,101},{6,102},{7,103},{8,104... | collective-permute-start | bytes 983048 | tf_op jit(solution)/shard_map/ppermute | solution.py:46
  170.2 1.2 collective-permute-done.22
  171.9 2.8 %collective-permute-start.23 = (f32[8,128]{1,0:T(8,128)S(1)}, f32[8,128]{1,0:T(8,128)S(1)}, u32[]{:S(2)}, u32[]{:S(2)}) collective-permute-start(f32[8,128]{1,0:T(8,128)S(1)} %add.18), channel_id=1, source_target_pairs={{0,16},{1,17},{2,18},{3,19},{4,20},{5,21},{6,22},{7,23},{8,24},{9,... | collective-permute-start | bytes 12296 | tf_op jit(solution)/shard_map/ppermute | solution.py:53
  174.7 2.2 %ring_add.3 = (bf16[160,1024]{1,0:T(8,128)(2,1)}, bf16[160,1024]{1,0:T(8,128)(2,1)}) custom-call(bf16[1280,1024]{1,0:T(8,128)(2,1)} %get-tuple-element.61.refs_0_.refs_2_, bf16[160,1024]{1,0:T(8,128)(2,1)} %collective-permute-done.34.refs_1_, bf16[1280,1024]{1,0:T(8,128)(2,1)} %get-tuple-element.61.refs_0_.refs_2_, ...), custom_call_target="tpu_custom_call" | custom-call | tf_op jit(solution)/shard_map/ring_add/pallas_call | solution.py:182
  176.9 2.7 %collective-permute-start.38 = (bf16[160,1024]{1,0:T(8,128)(2,1)}, bf16[160,1024]{1,0:T(8,128)(2,1)}, u32[]{:S(2)}, u32[]{:S(2)}) collective-permute-start(bf16[160,1024]{1,0:T(8,128)(2,1)} %get-tuple-element.67), channel_id=1, source_target_pairs={{0,6},{1,7},{2,0},{3,1},{4,2},{5,3},{6,4},{7,5},{8,14},{9,15},{10,... | collective-permute-start | bytes 983048 | tf_op jit(solution)/shard_map/ppermute | solution.py:46
  179.6 2.4 %ring_add.2 = (bf16[160,1024]{1,0:T(8,128)(2,1)}, bf16[160,1024]{1,0:T(8,128)(2,1)}) custom-call(bf16[1280,1024]{1,0:T(8,128)(2,1)} %get-tuple-element.52.refs_0_.refs_2_.refs_4_.refs_6_.refs_3_, bf16[1280,1024]{1,0:T(8,128)(2,1)} %collective-permute-done.24.refs_1_.refs_3_.refs_5_.refs_7_.refs_4_, bf16[160,1024]{1,0:T(8,128)(2,1)} %collective-permute-done.26.refs_2_, ...), custom_call_target="tpu_custom_call" | custom-call | tf_op jit(solution)/shard_map/ring_add/pallas_call | solution.py:182
  182.0 3.2 %collective-permute-start.30 = (bf16[160,1024]{1,0:T(8,128)(2,1)}, bf16[160,1024]{1,0:T(8,128)(2,1)}, u32[]{:S(2)}, u32[]{:S(2)}) collective-permute-start(bf16[160,1024]{1,0:T(8,128)(2,1)} %get-tuple-element.59), channel_id=1, source_target_pairs={{0,96},{1,97},{2,98},{3,99},{4,100},{5,101},{6,102},{7,103},{8,104... | collective-permute-start | bytes 983048 | tf_op jit(solution)/shard_map/ppermute | solution.py:46
  185.3 2.0 collective-permute-start.28
  187.3 3.0 %collective-permute-start.33 = (bf16[160,1024]{1,0:T(8,128)(2,1)}, bf16[160,1024]{1,0:T(8,128)(2,1)}, u32[]{:S(2)}, u32[]{:S(2)}) collective-permute-start(bf16[160,1024]{1,0:T(8,128)(2,1)} %get-tuple-element.62), channel_id=1, source_target_pairs={{0,6},{1,7},{2,0},{3,1},{4,2},{5,3},{6,4},{7,5},{8,14},{9,15},{10,... | collective-permute-start | bytes 983048 | tf_op jit(solution)/shard_map/ppermute | solution.py:46
  190.3 2.0 pair_sum.2
  192.4 1.4 collective-permute-done.30.refs_3_
  194.0 2.2 %pair_sum.3 = bf16[160,1024]{1,0:T(8,128)(2,1)} custom-call(bf16[1280,1024]{1,0:T(8,128)(2,1)} %get-tuple-element.52.refs_0_.refs_2_.refs_4_.refs_6_.refs_3_, bf16[1280,1024]{1,0:T(8,128)(2,1)} %collective-permute-done.24.refs_1_.refs_3_.refs_5_.refs_7_.refs_4_, bf16[160,1024]{1,0:T(8,128)(2,1)} %collective-permute-done.29.refs_2_, ...), custom_call_target="tpu_custom_call" | custom-call | tf_op jit(solution)/shard_map/pair_sum/pallas_call | solution.py:203
  196.1 2.7 %collective-permute-done.25.refs_2_ = bf16[160,1024]{1,0:T(8,128)(2,1)} collective-permute-done((bf16[160,1024]{1,0:T(8,128)(2,1)}, bf16[160,1024]{1,0:T(8,128)(2,1)}, u32[]{:S(2)}, u32[]{:S(2)}) %collective-permute-start.25) | collective-permute-done | bytes 327712 | tf_op jit(solution)/shard_map/ppermute | solution.py:46
  198.8 1.4 collective-permute-start.40
  200.2 3.6 %collective-permute-done.31 = f32[8,128]{1,0:T(8,128)S(1)} collective-permute-done((f32[8,128]{1,0:T(8,128)S(1)}, f32[8,128]{1,0:T(8,128)S(1)}, u32[]{:S(2)}, u32[]{:S(2)}) %collective-permute-start.31) | collective-permute-done | bytes 4128 | tf_op jit(solution)/shard_map/ppermute | solution.py:53
  203.8 3.2 %collective-permute-start.32 = (f32[8,128]{1,0:T(8,128)S(1)}, f32[8,128]{1,0:T(8,128)S(1)}, u32[]{:S(2)}, u32[]{:S(2)}) collective-permute-start(f32[8,128]{1,0:T(8,128)S(1)} %add.20), channel_id=1, source_target_pairs={{0,64},{1,65},{2,66},{3,67},{4,68},{5,69},{6,70},{7,71},{8,72},{9,... | collective-permute-start | bytes 12296 | tf_op jit(solution)/shard_map/ppermute | solution.py:53
  207.0 2.5 %finish.2 = bf16[160,1024]{1,0:T(8,128)(2,1)} custom-call(bf16[1280,1024]{1,0:T(8,128)(2,1)} %get-tuple-element.61.refs_0_.refs_2_, bf16[160,1024]{1,0:T(8,128)(2,1)} %collective-permute-done.33.refs_1_, bf16[160,1024]{1,0:T(8,128)(2,1)} %collective-permute-done.36.refs_2_, bf16[160,1024]{1,0:T(8,128)(2,1)} %collective-permute-done.39.refs_3_, ...), custom_call_target="tpu_custom_call" | custom-call | tf_op jit(solution)/shard_map/finish/pallas_call | solution.py:226
  210.7 2.6 %finish.3 = bf16[160,1024]{1,0:T(8,128)(2,1)} custom-call(bf16[1280,1024]{1,0:T(8,128)(2,1)} %get-tuple-element.52.refs_0_.refs_2_.refs_4_.refs_6_.refs_3_, bf16[1280,1024]{1,0:T(8,128)(2,1)} %collective-permute-done.24.refs_1_.refs_3_.refs_5_.refs_7_.refs_4_, bf16[160,1024]{1,0:T(8,128)(2,1)} %collective-permute-done.25.refs_2_, ...), custom_call_target="tpu_custom_call" | custom-call | tf_op jit(solution)/shard_map/finish/pallas_call | solution.py:226
  (64 shorter events, 9.1 us)
Async XLA Ops:
  0.6 13.1 %all-to-all-start = ((bf16[8,160,128]{2,1,0:T(8,128)(2,1)}), bf16[8,160,128]{2,1,0:T(8,128)(2,1)}, u32[]{:S(2)}, u32[]{:S(2)}) async-start(bf16[8,160,128]{2,1,0:T(8,128)(2,1)} %bitcast.4), calls=%async_computation | async-start | bytes 655360 | tf_op jit(solution)/shard_map/all_to_all | solution.py:611
  13.8 16.2 %collective-permute-start.2 = (bf16[320,1024]{1,0:T(8,128)(2,1)}, bf16[320,1024]{1,0:T(8,128)(2,1)}, u32[]{:S(2)}, u32[]{:S(2)}) collective-permute-start(bf16[320,1024]{1,0:T(8,128)(2,1)} %own_image.1.refs_0_), channel_id=1, source_target_pairs={{0,2},{1,3},{2,4},{3,5},{4,6},{5,7},{6,0},{7,1},{8,10},{9,11},{10,... | collective-permute-start | bytes 1966088 | tf_op jit(solution)/shard_map/ppermute | solution.py:46
  14.1 17.9 %collective-permute-start.1 = (bf16[320,1024]{1,0:T(8,128)(2,1)}, bf16[320,1024]{1,0:T(8,128)(2,1)}, u32[]{:S(2)}, u32[]{:S(2)}) collective-permute-start(bf16[320,1024]{1,0:T(8,128)(2,1)} %own_image.1.refs_0_), channel_id=1, source_target_pairs={{0,6},{1,7},{2,0},{3,1},{4,2},{5,3},{6,4},{7,5},{8,14},{9,15},{10,... | collective-permute-start | bytes 1966088 | tf_op jit(solution)/shard_map/ppermute | solution.py:46
  17.0 18.0 %collective-permute-start = (bf16[320,1024]{1,0:T(8,128)(2,1)}, bf16[320,1024]{1,0:T(8,128)(2,1)}, u32[]{:S(2)}, u32[]{:S(2)}) collective-permute-start(bf16[320,1024]{1,0:T(8,128)(2,1)} %own_image.1.refs_0_), channel_id=1, source_target_pairs={{0,1},{1,0},{2,3},{3,2},{4,5},{5,4},{6,7},{7,6},{8,9},{9,8},{10,11... | collective-permute-start | bytes 1966088 | tf_op jit(solution)/shard_map/ppermute | solution.py:46
  21.1 27.1 %collective-permute-start.7 = (bf16[320,1024]{1,0:T(8,128)(2,1)}, bf16[320,1024]{1,0:T(8,128)(2,1)}, u32[]{:S(2)}, u32[]{:S(2)}) collective-permute-start(bf16[320,1024]{1,0:T(8,128)(2,1)} %own_text.1.refs_8_.refs_1_), channel_id=1, source_target_pairs={{0,16},{1,17},{2,18},{3,19},{4,20},{5,21},{6,22},{7,23},{8,24},{9,... | collective-permute-start | bytes 1966088 | tf_op jit(solution)/shard_map/ppermute | solution.py:46
  24.0 24.2 %collective-permute-start.6 = (bf16[320,1024]{1,0:T(8,128)(2,1)}, bf16[320,1024]{1,0:T(8,128)(2,1)}, u32[]{:S(2)}, u32[]{:S(2)}) collective-permute-start(bf16[320,1024]{1,0:T(8,128)(2,1)} %own_text.1.refs_8_.refs_1_), channel_id=1, source_target_pairs={{0,96},{1,97},{2,98},{3,99},{4,100},{5,101},{6,102},{7,103},{8,104... | collective-permute-start | bytes 1966088 | tf_op jit(solution)/shard_map/ppermute | solution.py:46
  30.0 18.1 %collective-permute-start.5 = (bf16[320,1024]{1,0:T(8,128)(2,1)}, bf16[320,1024]{1,0:T(8,128)(2,1)}, u32[]{:S(2)}, u32[]{:S(2)}) collective-permute-start(bf16[320,1024]{1,0:T(8,128)(2,1)} %own_text.1.refs_8_.refs_1_), channel_id=1, source_target_pairs={{0,32},{1,33},{2,34},{3,35},{4,36},{5,37},{6,38},{7,39},{8,40},{9,... | collective-permute-start | bytes 1966088 | tf_op jit(solution)/shard_map/ppermute | solution.py:46
  35.0 17.3 %collective-permute-start.4 = (bf16[320,1024]{1,0:T(8,128)(2,1)}, bf16[320,1024]{1,0:T(8,128)(2,1)}, u32[]{:S(2)}, u32[]{:S(2)}) collective-permute-start(bf16[320,1024]{1,0:T(8,128)(2,1)} %collective-permute-done.refs_1_), channel_id=1, source_target_pairs={{0,2},{1,3},{2,4},{3,5},{4,6},{5,7},{6,0},{7,1},{8,10},{9,11},{10,... | collective-permute-start | bytes 1966088 | tf_op jit(solution)/shard_map/ppermute | solution.py:46
  35.0 17.3 %collective-permute-start.3 = (bf16[320,1024]{1,0:T(8,128)(2,1)}, bf16[320,1024]{1,0:T(8,128)(2,1)S(1)}, u32[]{:S(2)}, u32[]{:S(2)}) collective-permute-start(bf16[320,1024]{1,0:T(8,128)(2,1)} %collective-permute-done.refs_1_), channel_id=1, source_target_pairs={{0,6},{1,7},{2,0},{3,1},{4,2},{5,3},{6,4},{7,5},{8,14},{9,15},{10,... | collective-permute-start | bytes 1966088 | tf_op jit(solution)/shard_map/ppermute | solution.py:46
  48.2 16.4 %collective-permute-start.11 = (bf16[320,1024]{1,0:T(8,128)(2,1)}, bf16[320,1024]{1,0:T(8,128)(2,1)}, u32[]{:S(2)}, u32[]{:S(2)}) collective-permute-start(bf16[320,1024]{1,0:T(8,128)(2,1)} %collective-permute-done.7.refs_9_.refs_2_), channel_id=1, source_target_pairs={{0,32},{1,33},{2,34},{3,35},{4,36},{5,37},{6,38},{7,39},{8,40},{9,... | collective-permute-start | bytes 1966088 | tf_op jit(solution)/shard_map/ppermute | solution.py:46
  50.1 14.5 %collective-permute-start.10 = (bf16[320,1024]{1,0:T(8,128)(2,1)}, bf16[320,1024]{1,0:T(8,128)(2,1)}, u32[]{:S(2)}, u32[]{:S(2)}) collective-permute-start(bf16[320,1024]{1,0:T(8,128)(2,1)} %collective-permute-done.7.refs_9_.refs_2_), channel_id=1, source_target_pairs={{0,96},{1,97},{2,98},{3,99},{4,100},{5,101},{6,102},{7,103},{8,104... | collective-permute-start | bytes 1966088 | tf_op jit(solution)/shard_map/ppermute | solution.py:46
  52.3 0.8 copy-start
  52.3 15.5 %collective-permute-start.8 = (bf16[320,1024]{1,0:T(8,128)(2,1)}, bf16[320,1024]{1,0:T(8,128)(2,1)S(1)}, u32[]{:S(2)}, u32[]{:S(2)}) collective-permute-start(bf16[320,1024]{1,0:T(8,128)(2,1)} %collective-permute-done.2.refs_6_), channel_id=1, source_target_pairs={{0,2},{1,3},{2,4},{3,5},{4,6},{5,7},{6,0},{7,1},{8,10},{9,11},{10,... | collective-permute-start | bytes 1966088 | tf_op jit(solution)/shard_map/ppermute | solution.py:46
  53.1 15.2 %collective-permute-start.9 = (bf16[320,1024]{1,0:T(8,128)(2,1)S(1)}, bf16[320,1024]{1,0:T(8,128)(2,1)S(1)}, u32[]{:S(2)}, u32[]{:S(2)}) collective-permute-start(bf16[320,1024]{1,0:T(8,128)(2,1)S(1)} %collective-permute-done.3.refs_3_), channel_id=1, source_target_pairs={{0,6},{1,7},{2,0},{3,1},{4,2},{5,3},{6,4},{7,5},{8,14},{9,15},{10,... | collective-permute-start | bytes 1966088 | tf_op jit(solution)/shard_map/ppermute | solution.py:46
  64.6 14.7 %collective-permute-start.12 = (bf16[320,1024]{1,0:T(8,128)(2,1)}, bf16[320,1024]{1,0:T(8,128)(2,1)}, u32[]{:S(2)}, u32[]{:S(2)}) collective-permute-start(bf16[320,1024]{1,0:T(8,128)(2,1)} %collective-permute-done.5.refs_14_.refs_7_), channel_id=1, source_target_pairs={{0,32},{1,33},{2,34},{3,35},{4,36},{5,37},{6,38},{7,39},{8,40},{9,... | collective-permute-start | bytes 1966088 | tf_op jit(solution)/shard_map/ppermute | solution.py:46
  65.9 13.4 %collective-permute-start.13 = (bf16[320,1024]{1,0:T(8,128)(2,1)}, bf16[320,1024]{1,0:T(8,128)(2,1)}, u32[]{:S(2)}, u32[]{:S(2)}) collective-permute-start(bf16[320,1024]{1,0:T(8,128)(2,1)} %collective-permute-done.10.refs_11_.refs_4_), channel_id=1, source_target_pairs={{0,96},{1,97},{2,98},{3,99},{4,100},{5,101},{6,102},{7,103},{8,104... | collective-permute-start | bytes 1966088 | tf_op jit(solution)/shard_map/ppermute | solution.py:46
  67.8 12.0 %collective-permute-start.14 = (bf16[320,1024]{1,0:T(8,128)(2,1)}, bf16[320,1024]{1,0:T(8,128)(2,1)}, u32[]{:S(2)}, u32[]{:S(2)}) collective-permute-start(bf16[320,1024]{1,0:T(8,128)(2,1)} %own_text.1.refs_8_.refs_1_), channel_id=1, source_target_pairs={{0,8},{1,9},{2,10},{3,11},{4,12},{5,13},{6,14},{7,15},{8,0},{9,1},... | collective-permute-start | bytes 1966088 | tf_op jit(solution)/shard_map/ppermute | solution.py:46
  67.8 0.8 copy-start.1
  67.8 12.0 %collective-permute-start.15 = (bf16[320,1024]{1,0:T(8,128)(2,1)}, bf16[320,1024]{1,0:T(8,128)(2,1)}, u32[]{:S(2)}, u32[]{:S(2)}) collective-permute-start(bf16[320,1024]{1,0:T(8,128)(2,1)} %collective-permute-done.7.refs_9_.refs_2_), channel_id=1, source_target_pairs={{0,8},{1,9},{2,10},{3,11},{4,12},{5,13},{6,14},{7,15},{8,0},{9,1},... | collective-permute-start | bytes 1966088 | tf_op jit(solution)/shard_map/ppermute | solution.py:46
  68.7 0.8 copy-start.2
  69.5 10.8 %collective-permute-start.16 = (bf16[320,1024]{1,0:T(8,128)(2,1)}, bf16[320,1024]{1,0:T(8,128)(2,1)}, u32[]{:S(2)}, u32[]{:S(2)}) collective-permute-start(bf16[320,1024]{1,0:T(8,128)(2,1)} %collective-permute-done.6.refs_10_.refs_3_), channel_id=1, source_target_pairs={{0,8},{1,9},{2,10},{3,11},{4,12},{5,13},{6,14},{7,15},{8,0},{9,1},... | collective-permute-start | bytes 1966088 | tf_op jit(solution)/shard_map/ppermute | solution.py:46
  79.3 2.6 %collective-permute-start.20 = (bf16[320,1024]{1,0:T(8,128)(2,1)}, bf16[320,1024]{1,0:T(8,128)(2,1)}, u32[]{:S(2)}, u32[]{:S(2)}) collective-permute-start(bf16[320,1024]{1,0:T(8,128)(2,1)} %collective-permute-done.5.refs_14_.refs_7_), channel_id=1, source_target_pairs={{0,8},{1,9},{2,10},{3,11},{4,12},{5,13},{6,14},{7,15},{8,0},{9,1},... | collective-permute-start | bytes 1966088 | tf_op jit(solution)/shard_map/ppermute | solution.py:46
  79.3 3.4 %collective-permute-start.21 = (bf16[320,1024]{1,0:T(8,128)(2,1)}, bf16[320,1024]{1,0:T(8,128)(2,1)}, u32[]{:S(2)}, u32[]{:S(2)}) collective-permute-start(bf16[320,1024]{1,0:T(8,128)(2,1)} %collective-permute-done.11.refs_15_.refs_8_), channel_id=1, source_target_pairs={{0,8},{1,9},{2,10},{3,11},{4,12},{5,13},{6,14},{7,15},{8,0},{9,1},... | collective-permute-start | bytes 1966088 | tf_op jit(solution)/shard_map/ppermute | solution.py:46
  79.8 3.8 %collective-permute-start.17 = (bf16[320,1024]{1,0:T(8,128)(2,1)}, bf16[320,1024]{1,0:T(8,128)(2,1)}, u32[]{:S(2)}, u32[]{:S(2)}) collective-permute-start(bf16[320,1024]{1,0:T(8,128)(2,1)} %collective-permute-done.10.refs_11_.refs_4_), channel_id=1, source_target_pairs={{0,8},{1,9},{2,10},{3,11},{4,12},{5,13},{6,14},{7,15},{8,0},{9,1},... | collective-permute-start | bytes 1966088 | tf_op jit(solution)/shard_map/ppermute | solution.py:46
  79.9 4.6 %collective-permute-start.18 = (bf16[320,1024]{1,0:T(8,128)(2,1)}, bf16[320,1024]{1,0:T(8,128)(2,1)}, u32[]{:S(2)}, u32[]{:S(2)}) collective-permute-start(bf16[320,1024]{1,0:T(8,128)(2,1)} %collective-permute-done.12.refs_12_.refs_5_), channel_id=1, source_target_pairs={{0,8},{1,9},{2,10},{3,11},{4,12},{5,13},{6,14},{7,15},{8,0},{9,1},... | collective-permute-start | bytes 1966088 | tf_op jit(solution)/shard_map/ppermute | solution.py:46
  80.3 5.2 %collective-permute-start.19 = (bf16[320,1024]{1,0:T(8,128)(2,1)}, bf16[320,1024]{1,0:T(8,128)(2,1)}, u32[]{:S(2)}, u32[]{:S(2)}) collective-permute-start(bf16[320,1024]{1,0:T(8,128)(2,1)} %collective-permute-done.13.refs_13_.refs_6_), channel_id=1, source_target_pairs={{0,8},{1,9},{2,10},{3,11},{4,12},{5,13},{6,14},{7,15},{8,0},{9,1},... | collective-permute-start | bytes 1966088 | tf_op jit(solution)/shard_map/ppermute | solution.py:46
  158.8 5.3 %collective-permute-start.24 = (bf16[1280,1024]{1,0:T(8,128)(2,1)}, bf16[1280,1024]{1,0:T(8,128)(2,1)}, u32[]{:S(2)}, u32[]{:S(2)}) collective-permute-start(bf16[1280,1024]{1,0:T(8,128)(2,1)} %get-tuple-element.53), channel_id=1, source_target_pairs={{0,8},{1,9},{2,10},{3,11},{4,12},{5,13},{6,14},{7,15},{8,0},{9,1},... | collective-permute-start | bytes 7864328 | tf_op jit(solution)/shard_map/ppermute | solution.py:46
  158.9 13.0 %collective-permute-start.34 = (bf16[160,1024]{1,0:T(8,128)(2,1)}, bf16[160,1024]{1,0:T(8,128)(2,1)}, u32[]{:S(2)}, u32[]{:S(2)}) collective-permute-start(bf16[160,1024]{1,0:T(8,128)(2,1)} %get-tuple-element.63), channel_id=1, source_target_pairs={{0,2},{1,3},{2,4},{3,5},{4,6},{5,7},{6,0},{7,1},{8,10},{9,11},{10,... | collective-permute-start | bytes 983048 | tf_op jit(solution)/shard_map/ppermute | solution.py:46
  159.5 15.2 %collective-permute-start.35 = (bf16[160,1024]{1,0:T(8,128)(2,1)}, bf16[160,1024]{1,0:T(8,128)(2,1)}, u32[]{:S(2)}, u32[]{:S(2)}) collective-permute-start(bf16[160,1024]{1,0:T(8,128)(2,1)} %get-tuple-element.64), channel_id=1, source_target_pairs={{0,6},{1,7},{2,0},{3,1},{4,2},{5,3},{6,4},{7,5},{8,14},{9,15},{10,... | collective-permute-start | bytes 983048 | tf_op jit(solution)/shard_map/ppermute | solution.py:46
  164.1 6.1 %copy-start.3 = (f32[8,128]{1,0:T(8,128)S(1)}, f32[8,128]{1,0:T(8,128)}, u32[]{:S(2)}) copy-start(f32[8,128]{1,0:T(8,128)} %get-tuple-element.51) | copy-start | bytes 12292
  166.9 12.7 %collective-permute-start.26 = (bf16[160,1024]{1,0:T(8,128)(2,1)}, bf16[160,1024]{1,0:T(8,128)(2,1)}, u32[]{:S(2)}, u32[]{:S(2)}) collective-permute-start(bf16[160,1024]{1,0:T(8,128)(2,1)} %get-tuple-element.55), channel_id=1, source_target_pairs={{0,32},{1,33},{2,34},{3,35},{4,36},{5,37},{6,38},{7,39},{8,40},{9,... | collective-permute-start | bytes 983048 | tf_op jit(solution)/shard_map/ppermute | solution.py:46
  166.9 12.7 %collective-permute-start.27 = (bf16[160,1024]{1,0:T(8,128)(2,1)}, bf16[160,1024]{1,0:T(8,128)(2,1)}, u32[]{:S(2)}, u32[]{:S(2)}) collective-permute-start(bf16[160,1024]{1,0:T(8,128)(2,1)} %get-tuple-element.56), channel_id=1, source_target_pairs={{0,96},{1,97},{2,98},{3,99},{4,100},{5,101},{6,102},{7,103},{8,104... | collective-permute-start | bytes 983048 | tf_op jit(solution)/shard_map/ppermute | solution.py:46
  170.2 1.2 collective-permute-start.22
  171.3 14.0 %collective-permute-start.37 = (bf16[160,1024]{1,0:T(8,128)(2,1)}, bf16[160,1024]{1,0:T(8,128)(2,1)}, u32[]{:S(2)}, u32[]{:S(2)}) collective-permute-start(bf16[160,1024]{1,0:T(8,128)(2,1)} %get-tuple-element.66), channel_id=1, source_target_pairs={{0,2},{1,3},{2,4},{3,5},{4,6},{5,7},{6,0},{7,1},{8,10},{9,11},{10,... | collective-permute-start | bytes 983048 | tf_op jit(solution)/shard_map/ppermute | solution.py:46
  171.9 13.4 %collective-permute-start.23 = (f32[8,128]{1,0:T(8,128)S(1)}, f32[8,128]{1,0:T(8,128)S(1)}, u32[]{:S(2)}, u32[]{:S(2)}) collective-permute-start(f32[8,128]{1,0:T(8,128)S(1)} %add.18), channel_id=1, source_target_pairs={{0,16},{1,17},{2,18},{3,19},{4,20},{5,21},{6,22},{7,23},{8,24},{9,... | collective-permute-start | bytes 12296 | tf_op jit(solution)/shard_map/ppermute | solution.py:53
  176.9 10.4 %collective-permute-start.38 = (bf16[160,1024]{1,0:T(8,128)(2,1)}, bf16[160,1024]{1,0:T(8,128)(2,1)}, u32[]{:S(2)}, u32[]{:S(2)}) collective-permute-start(bf16[160,1024]{1,0:T(8,128)(2,1)} %get-tuple-element.67), channel_id=1, source_target_pairs={{0,6},{1,7},{2,0},{3,1},{4,2},{5,3},{6,4},{7,5},{8,14},{9,15},{10,... | collective-permute-start | bytes 983048 | tf_op jit(solution)/shard_map/ppermute | solution.py:46
  179.6 12.8 %collective-permute-start.29 = (bf16[160,1024]{1,0:T(8,128)(2,1)}, bf16[160,1024]{1,0:T(8,128)(2,1)}, u32[]{:S(2)}, u32[]{:S(2)}) collective-permute-start(bf16[160,1024]{1,0:T(8,128)(2,1)} %get-tuple-element.58), channel_id=1, source_target_pairs={{0,32},{1,33},{2,34},{3,35},{4,36},{5,37},{6,38},{7,39},{8,40},{9,... | collective-permute-start | bytes 983048 | tf_op jit(solution)/shard_map/ppermute | solution.py:46
  182.0 11.7 %collective-permute-start.30 = (bf16[160,1024]{1,0:T(8,128)(2,1)}, bf16[160,1024]{1,0:T(8,128)(2,1)}, u32[]{:S(2)}, u32[]{:S(2)}) collective-permute-start(bf16[160,1024]{1,0:T(8,128)(2,1)} %get-tuple-element.59), channel_id=1, source_target_pairs={{0,96},{1,97},{2,98},{3,99},{4,100},{5,101},{6,102},{7,103},{8,104... | collective-permute-start | bytes 983048 | tf_op jit(solution)/shard_map/ppermute | solution.py:46
  185.3 13.5 %collective-permute-start.25 = (bf16[160,1024]{1,0:T(8,128)(2,1)}, bf16[160,1024]{1,0:T(8,128)(2,1)}, u32[]{:S(2)}, u32[]{:S(2)}) collective-permute-start(bf16[160,1024]{1,0:T(8,128)(2,1)} %get-tuple-element.54), channel_id=1, source_target_pairs={{0,96},{1,97},{2,98},{3,99},{4,100},{5,101},{6,102},{7,103},{8,104... | collective-permute-start | bytes 983048 | tf_op jit(solution)/shard_map/ppermute | solution.py:46
  185.3 14.9 %collective-permute-start.28 = (bf16[160,1024]{1,0:T(8,128)(2,1)}, bf16[160,1024]{1,0:T(8,128)(2,1)}, u32[]{:S(2)}, u32[]{:S(2)}) collective-permute-start(bf16[160,1024]{1,0:T(8,128)(2,1)} %get-tuple-element.57), channel_id=1, source_target_pairs={{0,32},{1,33},{2,34},{3,35},{4,36},{5,37},{6,38},{7,39},{8,40},{9,... | collective-permute-start | bytes 983048 | tf_op jit(solution)/shard_map/ppermute | solution.py:46
  187.3 19.7 %collective-permute-start.33 = (bf16[160,1024]{1,0:T(8,128)(2,1)}, bf16[160,1024]{1,0:T(8,128)(2,1)}, u32[]{:S(2)}, u32[]{:S(2)}) collective-permute-start(bf16[160,1024]{1,0:T(8,128)(2,1)} %get-tuple-element.62), channel_id=1, source_target_pairs={{0,6},{1,7},{2,0},{3,1},{4,2},{5,3},{6,4},{7,5},{8,14},{9,15},{10,... | collective-permute-start | bytes 983048 | tf_op jit(solution)/shard_map/ppermute | solution.py:46
  192.3 14.6 %collective-permute-start.36 = (bf16[160,1024]{1,0:T(8,128)(2,1)}, bf16[160,1024]{1,0:T(8,128)(2,1)}, u32[]{:S(2)}, u32[]{:S(2)}) collective-permute-start(bf16[160,1024]{1,0:T(8,128)(2,1)} %get-tuple-element.65), channel_id=1, source_target_pairs={{0,2},{1,3},{2,4},{3,5},{4,6},{5,7},{6,0},{7,1},{8,10},{9,11},{10,... | collective-permute-start | bytes 983048 | tf_op jit(solution)/shard_map/ppermute | solution.py:46
  193.7 13.2 %collective-permute-start.39 = (bf16[160,1024]{1,0:T(8,128)(2,1)}, bf16[160,1024]{1,0:T(8,128)(2,1)}, u32[]{:S(2)}, u32[]{:S(2)}) collective-permute-start(bf16[160,1024]{1,0:T(8,128)(2,1)} %pair_sum.2), channel_id=1, source_target_pairs={{0,1},{1,0},{2,3},{3,2},{4,5},{5,4},{6,7},{7,6},{8,9},{9,8},{10,11... | collective-permute-start | bytes 983048 | tf_op jit(solution)/shard_map/ppermute | solution.py:46
  198.8 11.9 %collective-permute-start.40 = (bf16[160,1024]{1,0:T(8,128)(2,1)}, bf16[160,1024]{1,0:T(8,128)(2,1)}, u32[]{:S(2)}, u32[]{:S(2)}) collective-permute-start(bf16[160,1024]{1,0:T(8,128)(2,1)} %pair_sum.3), channel_id=1, source_target_pairs={{0,16},{1,17},{2,18},{3,19},{4,20},{5,21},{6,22},{7,23},{8,24},{9,... | collective-permute-start | bytes 983048 | tf_op jit(solution)/shard_map/ppermute | solution.py:46
  200.2 3.6 %collective-permute-start.31 = (f32[8,128]{1,0:T(8,128)S(1)}, f32[8,128]{1,0:T(8,128)S(1)}, u32[]{:S(2)}, u32[]{:S(2)}) collective-permute-start(f32[8,128]{1,0:T(8,128)S(1)} %add.19), channel_id=1, source_target_pairs={{0,32},{1,33},{2,34},{3,35},{4,36},{5,37},{6,38},{7,39},{8,40},{9,... | collective-permute-start | bytes 12296 | tf_op jit(solution)/shard_map/ppermute | solution.py:53
  203.8 5.7 %collective-permute-start.32 = (f32[8,128]{1,0:T(8,128)S(1)}, f32[8,128]{1,0:T(8,128)S(1)}, u32[]{:S(2)}, u32[]{:S(2)}) collective-permute-start(f32[8,128]{1,0:T(8,128)S(1)} %add.20), channel_id=1, source_target_pairs={{0,64},{1,65},{2,66},{3,67},{4,68},{5,69},{6,70},{7,71},{8,72},{9,... | collective-permute-start | bytes 12296 | tf_op jit(solution)/shard_map/ppermute | solution.py:53
where the time goes:
time: 216 us; the launch traced here: 214 us
  Pallas kernels  86.3 us (40%)
  starting transfers between devices  59.9 us (28%)
  waiting for transfers between devices  48.4 us (22%)
  blocking collectives  12.8 us (6%)
  between operations  3.84 us (2%)
  local copies, waits for them, and re-layouts  2.44 us (1%)
    ppermute x37, starting transfers between devices, send(): return lax.ppermute(value, AXES, perm=perm)  48.5 us
    ppermute x37, waiting for transfers between devices, send(): return lax.ppermute(value, AXES, perm=perm)  38.1 us
    pallas_call x1, Pallas kernels, grads(): pl.pallas_call(grads_kernel, grid=(steps,), out_shape=(shape((width // 2,...  26 us
    pallas_call x1, Pallas kernels, teacher_logits(): pl.pallas_call(teacher_kernel, grid=(width // COLS,), out_shape=(shape((r...  19 us
    pallas_call x1, Pallas kernels, student_logits(): pl.pallas_call(student_kernel, grid=(width // COLS,), out_shape=(shape((r...  15.4 us
    all_to_all x1, blocking collectives, on_device(): stats = lax.all_to_all(stats, 'loop', split_axis=0, concat_axis=0)  12.8 us
    ppermute x4, starting transfers between devices, swap_bit(): return lax.ppermute(value, AXES, perm=perm)  5.99 us
    all_to_all x1, waiting for transfers between devices, on_device(): lax.all_to_all(teacher_text.reshape(8, rows, -1), 'loop', split_axis=0, c...  5.58 us
  transfers between devices with their start and end apart: 42, of which 15 were waited for; matrix products, arithmetic and copies ran while one was open for 1% of the time, Pallas kernels for 11%

commit v1 on v0

--- a/solution.py
+++ b/solution.py
@@ -437,26 +437,33 @@
         cross = jnp.sum(ct[...] * shrink, axis=1, keepdims=True)
         lane = lax.broadcasted_iota(jnp.int32, ms.shape, 1)
         packed = jnp.zeros(ms.shape, F32)
-        for n, value in enumerate((smax, ssum, tmax, tsum, cross)):
+        values = (smax + jnp.log2(ssum), tmax + jnp.log2(tsum), cross / tsum)
+        for n, value in enumerate(values):
             packed = jnp.where(lane == n, value, packed)
+        turned = packed.T[:8, :]
+        count = turned.shape[1] // LANES
+        lines = [turned[n : n + 1, c * LANES : (c + 1) * LANES] for n in range(3) for c in range(count)]
+        lines.append(jnp.zeros((stats.shape[1] - 3 * count, LANES), F32))
+        block = jnp.concatenate(lines, axis=0)
         for n in range(8):
-            stats[n] = packed.T[:8, :]
+            stats[n] = block
 
 
 def teacher_logits(scale, image, texts, slog, ms, ss):
     rows, width = slog.shape
     code = image.shape[1]
+    lines = -(-(3 * rows // LANES + 1) // 8) * 8
     whole = pl.BlockSpec((rows, LANES), lambda i: (0, 0))
     return pl.pallas_call(
         teacher_kernel,
         grid=(width // COLS,),
-        out_shape=(shape((rows, width), F32), shape((8, 8, rows), F32)),
+        out_shape=(shape((rows, width), F32), shape((8, lines, LANES), F32)),
         in_specs=[SMEM, pl.BlockSpec((rows, code), lambda i: (0, 0))]
         + [ANY] * 16
         + [pl.BlockSpec((rows, COLS), lambda i: (0, i)), whole, whole],
         out_specs=(
             pl.BlockSpec((rows, COLS), lambda i: (0, i)),
-            pl.BlockSpec((8, 8, rows), lambda i: (0, 0, 0)),
+            pl.BlockSpec((8, lines, LANES), lambda i: (0, 0, 0)),
         ),
         scratch_shapes=[
             pltpu.VMEM((width, code), BF16),
@@ -474,17 +481,20 @@
 
 
 def merge_stats(stats, lses, lset, loss):
-    smax = jnp.max(stats[:, 0, :], axis=0, keepdims=True)
-    ssum = jnp.sum(stats[:, 1, :] * jnp.exp2(stats[:, 0, :] - smax), axis=0, keepdims=True)
-    tmax = jnp.max(stats[:, 2, :], axis=0, keepdims=True)
-    shrink = jnp.exp2(stats[:, 2, :] - tmax)
-    tsum = jnp.sum(stats[:, 3, :] * shrink, axis=0, keepdims=True)
-    cross = jnp.sum(stats[:, 4, :] * shrink, axis=0, keepdims=True)
-    lse_s = smax + jnp.log2(ssum)
+    rows = lses.shape[0]
+    count = rows // LANES
+    part_s, part_t, ratio = [
+        jnp.concatenate([stats[:, n * count + c, :] for c in range(count)], axis=1) for n in range(3)
+    ]
+    smax = jnp.max(part_s, axis=0, keepdims=True)
+    lse_s = smax + jnp.log2(jnp.sum(jnp.exp2(part_s - smax), axis=0, keepdims=True))
+    tmax = jnp.max(part_t, axis=0, keepdims=True)
+    weight = jnp.exp2(part_t - tmax)
+    tsum = jnp.sum(weight, axis=0, keepdims=True)
+    cross = jnp.sum(ratio * weight, axis=0, keepdims=True)
     lse_t = tmax + jnp.log2(tsum)
     diverge = LN2 * (cross / tsum - lse_t + lse_s)
     loss[...] = jnp.full(loss.shape, jnp.sum(diverge), F32)
-    rows = stats.shape[2]
     lses[...] = jnp.broadcast_to(lse_s, (LANES, rows)).T
     lset[...] = jnp.broadcast_to(lse_t, (LANES, rows)).T
 

time: 216 us -> 214 us (level)
  no operation moved by 1% of the time
where the time goes in v1:
time: 214 us; the launch traced here: 212 us
  Pallas kernels  86.3 us (40%)
  starting transfers between devices  60.1 us (28%)
  waiting for transfers between devices  48.2 us (23%)
  blocking collectives  10.9 us (5%)
  between operations  3.84 us (2%)
  local copies, waits for them, and re-layouts  2.44 us (1%)
    ppermute x37, starting transfers between devices, send(): return lax.ppermute(value, AXES, perm=perm)  48.7 us
    ppermute x37, waiting for transfers between devices, send(): return lax.ppermute(value, AXES, perm=perm)  37.9 us
    pallas_call x1, Pallas kernels, grads(): pl.pallas_call(grads_kernel, grid=(steps,), out_shape=(shape((width // 2,...  26 us
    pallas_call x1, Pallas kernels, teacher_logits(): pl.pallas_call(teacher_kernel, grid=(width // COLS,), out_shape=(shape((r...  19 us
    pallas_call x1, Pallas kernels, student_logits(): pl.pallas_call(student_kernel, grid=(width // COLS,), out_shape=(shape((r...  15.4 us
    all_to_all x1, blocking collectives, on_device(): stats = lax.all_to_all(stats, 'loop', split_axis=0, concat_axis=0)  10.9 us
    ppermute x4, starting transfers between devices, swap_bit(): return lax.ppermute(value, AXES, perm=perm)  5.97 us
    all_to_all x1, waiting for transfers between devices, on_device(): lax.all_to_all(teacher_text.reshape(8, rows, -1), 'loop', split_axis=0, c...  5.58 us
  transfers between devices with their start and end apart: 42, of which 15 were waited for; matrix products, arithmetic and copies ran while one was open for 1% of the time, Pallas kernels for 11%

profile of v1, /device:TPU:0, one launch (start us, length us, event | category | flops | bytes accessed | tf_op | source)
XLA Modules:
  0.0 212.5 jit_solution(7137243147460942123)
XLA Ops:
  0.6 5.4 %all-to-all-start = ((bf16[8,160,128]{2,1,0:T(8,128)(2,1)}), bf16[8,160,128]{2,1,0:T(8,128)(2,1)}, u32[]{:S(2)}, u32[]{:S(2)}) async-start(bf16[8,160,128]{2,1,0:T(8,128)(2,1)} %bitcast.4), calls=%async_computation | async-start | bytes 655360 | tf_op jit(solution)/shard_map/all_to_all | solution.py:621
  6.0 2.2 %own_image.1.refs_0_ = bf16[320,1024]{1,0:T(8,128)(2,1)} custom-call(bf16[160,1024]{1,0:T(8,128)(2,1)} %refs_4_.1, bf16[1280,128]{1,0:T(8,128)(2,1)} %ti.1), custom_call_target="tpu_custom_call" | custom-call | tf_op jit(solution)/shard_map/own_image/pallas_call | solution.py:87
  8.2 5.6 %all-to-all-done.parts = bf16[8,160,128]{2,1,0:T(8,128)(2,1)} async-done(((bf16[8,160,128]{2,1,0:T(8,128)(2,1)}), bf16[8,160,128]{2,1,0:T(8,128)(2,1)}, u32[]{:S(2)}, u32[]{:S(2)}) %all-to-all-start) | async-done | bytes 327712 | tf_op jit(solution)/shard_map/all_to_all | solution.py:621
  14.1 2.9 %collective-permute-start.1 = (bf16[320,1024]{1,0:T(8,128)(2,1)}, bf16[320,1024]{1,0:T(8,128)(2,1)}, u32[]{:S(2)}, u32[]{:S(2)}) collective-permute-start(bf16[320,1024]{1,0:T(8,128)(2,1)} %own_image.1.refs_0_), channel_id=1, source_target_pairs={{0,6},{1,7},{2,0},{3,1},{4,2},{5,3},{6,4},{7,5},{8,14},{9,15},{10,... | collective-permute-start | bytes 1966088 | tf_op jit(solution)/shard_map/ppermute | solution.py:46
  17.0 1.2 collective-permute-start
  18.8 2.2 %own_text.1.refs_8_.refs_1_ = bf16[320,1024]{1,0:T(8,128)(2,1)} custom-call(s32[2]{0:T(128)} %pad_add_fusion.where, bf16[160,1024]{1,0:T(8,128)(2,1)} %refs_5_.1, bf16[8,160,128]{2,1,0:T(8,128)(2,1)} %all-to-all-done.parts), custom_call_target="tpu_custom_call" | custom-call | tf_op jit(solution)/shard_map/own_text/pallas_call | solution.py:106
  21.0 2.9 %collective-permute-start.7 = (bf16[320,1024]{1,0:T(8,128)(2,1)}, bf16[320,1024]{1,0:T(8,128)(2,1)}, u32[]{:S(2)}, u32[]{:S(2)}) collective-permute-start(bf16[320,1024]{1,0:T(8,128)(2,1)} %own_text.1.refs_8_.refs_1_), channel_id=1, source_target_pairs={{0,16},{1,17},{2,18},{3,19},{4,20},{5,21},{6,22},{7,23},{8,24},{9,... | collective-permute-start | bytes 1966088 | tf_op jit(solution)/shard_map/ppermute | solution.py:46
  23.9 4.0 %collective-permute-start.6 = (bf16[320,1024]{1,0:T(8,128)(2,1)}, bf16[320,1024]{1,0:T(8,128)(2,1)}, u32[]{:S(2)}, u32[]{:S(2)}) collective-permute-start(bf16[320,1024]{1,0:T(8,128)(2,1)} %own_text.1.refs_8_.refs_1_), channel_id=1, source_target_pairs={{0,96},{1,97},{2,98},{3,99},{4,100},{5,101},{6,102},{7,103},{8,104... | collective-permute-start | bytes 1966088 | tf_op jit(solution)/shard_map/ppermute | solution.py:46
  28.0 2.1 collective-permute-done.2.refs_6_
  30.0 1.9 collective-permute-start.5
  31.9 3.1 %collective-permute-done.refs_1_ = bf16[320,1024]{1,0:T(8,128)(2,1)} collective-permute-done((bf16[320,1024]{1,0:T(8,128)(2,1)}, bf16[320,1024]{1,0:T(8,128)(2,1)}, u32[]{:S(2)}, u32[]{:S(2)}) %collective-permute-start) | collective-permute-done | bytes 655392 | tf_op jit(solution)/shard_map/ppermute | solution.py:46
  35.0 3.2 %collective-permute-start.3 = (bf16[320,1024]{1,0:T(8,128)(2,1)}, bf16[320,1024]{1,0:T(8,128)(2,1)S(1)}, u32[]{:S(2)}, u32[]{:S(2)}) collective-permute-start(bf16[320,1024]{1,0:T(8,128)(2,1)} %collective-permute-done.refs_1_), channel_id=1, source_target_pairs={{0,6},{1,7},{2,0},{3,1},{4,2},{5,3},{6,4},{7,5},{8,14},{9,15},{10,... | collective-permute-start | bytes 1966088 | tf_op jit(solution)/shard_map/ppermute | solution.py:46
  38.2 9.9 %collective-permute-done.7.refs_9_.refs_2_ = bf16[320,1024]{1,0:T(8,128)(2,1)} collective-permute-done((bf16[320,1024]{1,0:T(8,128)(2,1)}, bf16[320,1024]{1,0:T(8,128)(2,1)}, u32[]{:S(2)}, u32[]{:S(2)}) %collective-permute-start.7) | collective-permute-done | bytes 655392 | tf_op jit(solution)/shard_map/ppermute | solution.py:46
  48.2 1.9 collective-permute-start.11
  50.1 2.2 %collective-permute-start.10 = (bf16[320,1024]{1,0:T(8,128)(2,1)}, bf16[320,1024]{1,0:T(8,128)(2,1)}, u32[]{:S(2)}, u32[]{:S(2)}) collective-permute-start(bf16[320,1024]{1,0:T(8,128)(2,1)} %collective-permute-done.7.refs_9_.refs_2_), channel_id=1, source_target_pairs={{0,96},{1,97},{2,98},{3,99},{4,100},{5,101},{6,102},{7,103},{8,104... | collective-permute-start | bytes 1966088 | tf_op jit(solution)/shard_map/ppermute | solution.py:46
  53.1 2.5 %collective-permute-start.9 = (bf16[320,1024]{1,0:T(8,128)(2,1)S(1)}, bf16[320,1024]{1,0:T(8,128)(2,1)S(1)}, u32[]{:S(2)}, u32[]{:S(2)}) collective-permute-start(bf16[320,1024]{1,0:T(8,128)(2,1)S(1)} %collective-permute-done.3.refs_3_), channel_id=1, source_target_pairs={{0,6},{1,7},{2,0},{3,1},{4,2},{5,3},{6,4},{7,5},{8,14},{9,15},{10,... | collective-permute-start | bytes 1966088 | tf_op jit(solution)/shard_map/ppermute | solution.py:46
  55.6 9.0 %collective-permute-done.11.refs_15_.refs_8_ = bf16[320,1024]{1,0:T(8,128)(2,1)} collective-permute-done((bf16[320,1024]{1,0:T(8,128)(2,1)}, bf16[320,1024]{1,0:T(8,128)(2,1)}, u32[]{:S(2)}, u32[]{:S(2)}) %collective-permute-start.11) | collective-permute-done | bytes 655392 | tf_op jit(solution)/shard_map/ppermute | solution.py:46
  64.6 1.3 collective-permute-start.12
  65.9 2.0 collective-permute-start.13
  70.0 4.8 %teacher_images.1.refs_0_ = bf16[1280,1024]{1,0:T(8,128)(2,1)} custom-call(bf16[320,1024]{1,0:T(8,128)(2,1)} %own_image.1.refs_0_, bf16[320,1024]{1,0:T(8,128)(2,1)} %collective-permute-done.refs_1_, bf16[320,1024]{1,0:T(8,128)(2,1)} %collective-permute-done.1.refs_2_, bf16[320,1024]{1,0:T(8,128)(2,1)} %copy-done, bf16[320,1024]{1,0:T(8,128)(2,1)} %copy-done.1, ...), custom_call_target="tpu_custom_call" | custom-call | tf_op jit(solution)/shard_map/teacher_images/pallas_call | solution.py:377
  74.8 4.4 %collective-permute-done.12.refs_12_.refs_5_ = bf16[320,1024]{1,0:T(8,128)(2,1)} collective-permute-done((bf16[320,1024]{1,0:T(8,128)(2,1)}, bf16[320,1024]{1,0:T(8,128)(2,1)}, u32[]{:S(2)}, u32[]{:S(2)}) %collective-permute-start.12) | collective-permute-done | bytes 655392 | tf_op jit(solution)/shard_map/ppermute | solution.py:46
  82.7 0.9 collective-permute-done.17.refs_19_.refs_12_
  84.5 0.9 collective-permute-done.19.refs_21_.refs_14_
  85.5 15.4 %student_logits.1 = (f32[1280,2560]{1,0:T(8,128)}, f32[1280,128]{1,0:T(8,128)}, f32[1280,128]{1,0:T(8,128)}) custom-call(s32[2]{0:T(128)} %pad_add_fusion.where, f32[1]{0:T(128)S(6)} %copy.9.scale, bf16[320,1024]{1,0:T(8,128)(2,1)} %own_image.1.refs_0_, bf16[320,1024]{1,0:T(8,128)(2,1)} %collective-permute-done.refs_1_, ...), custom_call_target="tpu_custom_call" | custom-call | flops 6710886400 | bytes 13107200 | tf_op jit(solution)/shard_map/student_logits/pallas_call | solution.py:322
  100.9 19.0 %teacher_logits.1 = (f32[1280,2560]{1,0:T(8,128)}, f32[8,32,128]{2,1,0:T(8,128)}) custom-call(f32[1]{0:T(128)S(6)} %copy.10.scale, bf16[1280,1024]{1,0:T(8,128)(2,1)} %teacher_images.1.refs_0_, bf16[320,1024]{1,0:T(8,128)(2,1)} %own_text.1.refs_8_.refs_1_, bf16[320,1024]{1,0:T(8,128)(2,1)} %collective-permute-done.7.refs_9_.refs_2_, ...), custom_call_target="tpu_custom_call" | custom-call | flops 6710886400 | bytes 26214400 | tf_op jit(solution)/shard_map/teacher_logits/pallas_call | solution.py:457
  119.9 10.9 %all_to_all.10.refs_26_ = f32[8,32,128]{2,1,0:T(8,128)} all-to-all(f32[8,32,128]{2,1,0:T(8,128)} %get-tuple-element.50), channel_id=1, replica_groups=mesh['row'=16,'loop'=8] {'loop'}, dimensions={0} | all-to-all | bytes 262144 | tf_op jit(solution)/shard_map/all_to_all | solution.py:639
  130.9 26.0 %grads.1 = (bf16[1280,1024]{1,0:T(8,128)(2,1)}, bf16[1280,1024]{1,0:T(8,128)(2,1)}, bf16[1280,1024]{1,0:T(8,128)(2,1)}, bf16[160,1024]{1,0:T(8,128)(2,1)}, bf16[...) custom-call(s32[2]{0:T(128)} %pad_add_fusion.where, ...), custom_call_target="tpu_custom_call" | custom-call | flops 13421772800 | bytes 26214400 | tf_op jit(solution)/shard_map/grads/pallas_call | solution.py:575
  157.5 2.7 %collective-permute-start.35 = (bf16[160,1024]{1,0:T(8,128)(2,1)}, bf16[160,1024]{1,0:T(8,128)(2,1)}, u32[]{:S(2)}, u32[]{:S(2)}) collective-permute-start(bf16[160,1024]{1,0:T(8,128)(2,1)} %get-tuple-element.64), channel_id=1, source_target_pairs={{0,6},{1,7},{2,0},{3,1},{4,2},{5,3},{6,4},{7,5},{8,14},{9,15},{10,... | collective-permute-start | bytes 983048 | tf_op jit(solution)/shard_map/ppermute | solution.py:46
  160.2 1.9 collective-permute-done.24.refs_1_.refs_3_.refs_5_.refs_7_.refs_4_
  162.2 2.8 %early_sum.1 = (bf16[160,1024]{1,0:T(8,128)(2,1)}, bf16[160,1024]{1,0:T(8,128)(2,1)}, bf16[160,1024]{1,0:T(8,128)(2,1)}, bf16[160,1024]{1,0:T(8,128)(2,1)}) custom-call(bf16[1280,1024]{1,0:T(8,128)(2,1)} %get-tuple-element.52.refs_0_.refs_2_.refs_4_.refs_6_.refs_3_, bf16[1280,1024]{1,0:T(8,128)(2,1)} %collective-permute-done.24.refs_1_.refs_3_.refs_5_.refs_7_.refs_4_, ...), custom_call_target="tpu_custom_call" | custom-call | tf_op jit(solution)/shard_map/early_sum/pallas_call | solution.py:161
  165.0 3.2 %collective-permute-start.27 = (bf16[160,1024]{1,0:T(8,128)(2,1)}, bf16[160,1024]{1,0:T(8,128)(2,1)}, u32[]{:S(2)}, u32[]{:S(2)}) collective-permute-start(bf16[160,1024]{1,0:T(8,128)(2,1)} %get-tuple-element.56), channel_id=1, source_target_pairs={{0,96},{1,97},{2,98},{3,99},{4,100},{5,101},{6,102},{7,103},{8,104... | collective-permute-start | bytes 983048 | tf_op jit(solution)/shard_map/ppermute | solution.py:46
  168.2 1.2 collective-permute-done.22
  169.9 2.8 %collective-permute-start.23 = (f32[8,128]{1,0:T(8,128)S(1)}, f32[8,128]{1,0:T(8,128)S(1)}, u32[]{:S(2)}, u32[]{:S(2)}) collective-permute-start(f32[8,128]{1,0:T(8,128)S(1)} %add.18), channel_id=1, source_target_pairs={{0,16},{1,17},{2,18},{3,19},{4,20},{5,21},{6,22},{7,23},{8,24},{9,... | collective-permute-start | bytes 12296 | tf_op jit(solution)/shard_map/ppermute | solution.py:53
  172.7 2.2 %ring_add.3 = (bf16[160,1024]{1,0:T(8,128)(2,1)}, bf16[160,1024]{1,0:T(8,128)(2,1)}) custom-call(bf16[1280,1024]{1,0:T(8,128)(2,1)} %get-tuple-element.61.refs_0_.refs_2_, bf16[160,1024]{1,0:T(8,128)(2,1)} %collective-permute-done.34.refs_1_, bf16[1280,1024]{1,0:T(8,128)(2,1)} %get-tuple-element.61.refs_0_.refs_2_, ...), custom_call_target="tpu_custom_call" | custom-call | tf_op jit(solution)/shard_map/ring_add/pallas_call | solution.py:182
  174.9 2.7 %collective-permute-start.38 = (bf16[160,1024]{1,0:T(8,128)(2,1)}, bf16[160,1024]{1,0:T(8,128)(2,1)}, u32[]{:S(2)}, u32[]{:S(2)}) collective-permute-start(bf16[160,1024]{1,0:T(8,128)(2,1)} %get-tuple-element.67), channel_id=1, source_target_pairs={{0,6},{1,7},{2,0},{3,1},{4,2},{5,3},{6,4},{7,5},{8,14},{9,15},{10,... | collective-permute-start | bytes 983048 | tf_op jit(solution)/shard_map/ppermute | solution.py:46
  177.6 2.4 %ring_add.2 = (bf16[160,1024]{1,0:T(8,128)(2,1)}, bf16[160,1024]{1,0:T(8,128)(2,1)}) custom-call(bf16[1280,1024]{1,0:T(8,128)(2,1)} %get-tuple-element.52.refs_0_.refs_2_.refs_4_.refs_6_.refs_3_, bf16[1280,1024]{1,0:T(8,128)(2,1)} %collective-permute-done.24.refs_1_.refs_3_.refs_5_.refs_7_.refs_4_, bf16[160,1024]{1,0:T(8,128)(2,1)} %collective-permute-done.26.refs_2_, ...), custom_call_target="tpu_custom_call" | custom-call | tf_op jit(solution)/shard_map/ring_add/pallas_call | solution.py:182
  180.1 3.2 %collective-permute-start.30 = (bf16[160,1024]{1,0:T(8,128)(2,1)}, bf16[160,1024]{1,0:T(8,128)(2,1)}, u32[]{:S(2)}, u32[]{:S(2)}) collective-permute-start(bf16[160,1024]{1,0:T(8,128)(2,1)} %get-tuple-element.59), channel_id=1, source_target_pairs={{0,96},{1,97},{2,98},{3,99},{4,100},{5,101},{6,102},{7,103},{8,104... | collective-permute-start | bytes 983048 | tf_op jit(solution)/shard_map/ppermute | solution.py:46
  183.4 2.0 collective-permute-start.28
  185.3 3.0 %collective-permute-start.33 = (bf16[160,1024]{1,0:T(8,128)(2,1)}, bf16[160,1024]{1,0:T(8,128)(2,1)}, u32[]{:S(2)}, u32[]{:S(2)}) collective-permute-start(bf16[160,1024]{1,0:T(8,128)(2,1)} %get-tuple-element.62), channel_id=1, source_target_pairs={{0,6},{1,7},{2,0},{3,1},{4,2},{5,3},{6,4},{7,5},{8,14},{9,15},{10,... | collective-permute-start | bytes 983048 | tf_op jit(solution)/shard_map/ppermute | solution.py:46
  188.4 2.0 pair_sum.2
  190.4 1.4 collective-permute-done.30.refs_3_
  192.2 2.2 %pair_sum.3 = bf16[160,1024]{1,0:T(8,128)(2,1)} custom-call(bf16[1280,1024]{1,0:T(8,128)(2,1)} %get-tuple-element.52.refs_0_.refs_2_.refs_4_.refs_6_.refs_3_, bf16[1280,1024]{1,0:T(8,128)(2,1)} %collective-permute-done.24.refs_1_.refs_3_.refs_5_.refs_7_.refs_4_, bf16[160,1024]{1,0:T(8,128)(2,1)} %collective-permute-done.29.refs_2_, ...), custom_call_target="tpu_custom_call" | custom-call | tf_op jit(solution)/shard_map/pair_sum/pallas_call | solution.py:203
  194.4 2.5 %collective-permute-done.25.refs_2_ = bf16[160,1024]{1,0:T(8,128)(2,1)} collective-permute-done((bf16[160,1024]{1,0:T(8,128)(2,1)}, bf16[160,1024]{1,0:T(8,128)(2,1)}, u32[]{:S(2)}, u32[]{:S(2)}) %collective-permute-start.25) | collective-permute-done | bytes 327712 | tf_op jit(solution)/shard_map/ppermute | solution.py:46
  196.8 1.4 collective-permute-start.40
  198.2 3.6 %collective-permute-done.31 = f32[8,128]{1,0:T(8,128)S(1)} collective-permute-done((f32[8,128]{1,0:T(8,128)S(1)}, f32[8,128]{1,0:T(8,128)S(1)}, u32[]{:S(2)}, u32[]{:S(2)}) %collective-permute-start.31) | collective-permute-done | bytes 4128 | tf_op jit(solution)/shard_map/ppermute | solution.py:53
  201.8 3.2 %collective-permute-start.32 = (f32[8,128]{1,0:T(8,128)S(1)}, f32[8,128]{1,0:T(8,128)S(1)}, u32[]{:S(2)}, u32[]{:S(2)}) collective-permute-start(f32[8,128]{1,0:T(8,128)S(1)} %add.20), channel_id=1, source_target_pairs={{0,64},{1,65},{2,66},{3,67},{4,68},{5,69},{6,70},{7,71},{8,72},{9,... | collective-permute-start | bytes 12296 | tf_op jit(solution)/shard_map/ppermute | solution.py:53
  205.0 2.5 %finish.2 = bf16[160,1024]{1,0:T(8,128)(2,1)} custom-call(bf16[1280,1024]{1,0:T(8,128)(2,1)} %get-tuple-element.61.refs_0_.refs_2_, bf16[160,1024]{1,0:T(8,128)(2,1)} %collective-permute-done.33.refs_1_, bf16[160,1024]{1,0:T(8,128)(2,1)} %collective-permute-done.36.refs_2_, bf16[160,1024]{1,0:T(8,128)(2,1)} %collective-permute-done.39.refs_3_, ...), custom_call_target="tpu_custom_call" | custom-call | tf_op jit(solution)/shard_map/finish/pallas_call | solution.py:226
  208.7 2.6 %finish.3 = bf16[160,1024]{1,0:T(8,128)(2,1)} custom-call(bf16[1280,1024]{1,0:T(8,128)(2,1)} %get-tuple-element.52.refs_0_.refs_2_.refs_4_.refs_6_.refs_3_, bf16[1280,1024]{1,0:T(8,128)(2,1)} %collective-permute-done.24.refs_1_.refs_3_.refs_5_.refs_7_.refs_4_, bf16[160,1024]{1,0:T(8,128)(2,1)} %collective-permute-done.25.refs_2_, ...), custom_call_target="tpu_custom_call" | custom-call | tf_op jit(solution)/shard_map/finish/pallas_call | solution.py:226
  (64 shorter events, 9.2 us)
Async XLA Ops:
  0.6 13.1 %all-to-all-start = ((bf16[8,160,128]{2,1,0:T(8,128)(2,1)}), bf16[8,160,128]{2,1,0:T(8,128)(2,1)}, u32[]{:S(2)}, u32[]{:S(2)}) async-start(bf16[8,160,128]{2,1,0:T(8,128)(2,1)} %bitcast.4), calls=%async_computation | async-start | bytes 655360 | tf_op jit(solution)/shard_map/all_to_all | solution.py:621
  13.8 16.2 %collective-permute-start.2 = (bf16[320,1024]{1,0:T(8,128)(2,1)}, bf16[320,1024]{1,0:T(8,128)(2,1)}, u32[]{:S(2)}, u32[]{:S(2)}) collective-permute-start(bf16[320,1024]{1,0:T(8,128)(2,1)} %own_image.1.refs_0_), channel_id=1, source_target_pairs={{0,2},{1,3},{2,4},{3,5},{4,6},{5,7},{6,0},{7,1},{8,10},{9,11},{10,... | collective-permute-start | bytes 1966088 | tf_op jit(solution)/shard_map/ppermute | solution.py:46
  14.1 17.9 %collective-permute-start.1 = (bf16[320,1024]{1,0:T(8,128)(2,1)}, bf16[320,1024]{1,0:T(8,128)(2,1)}, u32[]{:S(2)}, u32[]{:S(2)}) collective-permute-start(bf16[320,1024]{1,0:T(8,128)(2,1)} %own_image.1.refs_0_), channel_id=1, source_target_pairs={{0,6},{1,7},{2,0},{3,1},{4,2},{5,3},{6,4},{7,5},{8,14},{9,15},{10,... | collective-permute-start | bytes 1966088 | tf_op jit(solution)/shard_map/ppermute | solution.py:46
  17.0 18.0 %collective-permute-start = (bf16[320,1024]{1,0:T(8,128)(2,1)}, bf16[320,1024]{1,0:T(8,128)(2,1)}, u32[]{:S(2)}, u32[]{:S(2)}) collective-permute-start(bf16[320,1024]{1,0:T(8,128)(2,1)} %own_image.1.refs_0_), channel_id=1, source_target_pairs={{0,1},{1,0},{2,3},{3,2},{4,5},{5,4},{6,7},{7,6},{8,9},{9,8},{10,11... | collective-permute-start | bytes 1966088 | tf_op jit(solution)/shard_map/ppermute | solution.py:46
  21.0 27.1 %collective-permute-start.7 = (bf16[320,1024]{1,0:T(8,128)(2,1)}, bf16[320,1024]{1,0:T(8,128)(2,1)}, u32[]{:S(2)}, u32[]{:S(2)}) collective-permute-start(bf16[320,1024]{1,0:T(8,128)(2,1)} %own_text.1.refs_8_.refs_1_), channel_id=1, source_target_pairs={{0,16},{1,17},{2,18},{3,19},{4,20},{5,21},{6,22},{7,23},{8,24},{9,... | collective-permute-start | bytes 1966088 | tf_op jit(solution)/shard_map/ppermute | solution.py:46
  23.9 24.2 %collective-permute-start.6 = (bf16[320,1024]{1,0:T(8,128)(2,1)}, bf16[320,1024]{1,0:T(8,128)(2,1)}, u32[]{:S(2)}, u32[]{:S(2)}) collective-permute-start(bf16[320,1024]{1,0:T(8,128)(2,1)} %own_text.1.refs_8_.refs_1_), channel_id=1, source_target_pairs={{0,96},{1,97},{2,98},{3,99},{4,100},{5,101},{6,102},{7,103},{8,104... | collective-permute-start | bytes 1966088 | tf_op jit(solution)/shard_map/ppermute | solution.py:46
  30.0 18.1 %collective-permute-start.5 = (bf16[320,1024]{1,0:T(8,128)(2,1)}, bf16[320,1024]{1,0:T(8,128)(2,1)}, u32[]{:S(2)}, u32[]{:S(2)}) collective-permute-start(bf16[320,1024]{1,0:T(8,128)(2,1)} %own_text.1.refs_8_.refs_1_), channel_id=1, source_target_pairs={{0,32},{1,33},{2,34},{3,35},{4,36},{5,37},{6,38},{7,39},{8,40},{9,... | collective-permute-start | bytes 1966088 | tf_op jit(solution)/shard_map/ppermute | solution.py:46
  35.0 17.3 %collective-permute-start.4 = (bf16[320,1024]{1,0:T(8,128)(2,1)}, bf16[320,1024]{1,0:T(8,128)(2,1)}, u32[]{:S(2)}, u32[]{:S(2)}) collective-permute-start(bf16[320,1024]{1,0:T(8,128)(2,1)} %collective-permute-done.refs_1_), channel_id=1, source_target_pairs={{0,2},{1,3},{2,4},{3,5},{4,6},{5,7},{6,0},{7,1},{8,10},{9,11},{10,... | collective-permute-start | bytes 1966088 | tf_op jit(solution)/shard_map/ppermute | solution.py:46
  35.0 17.3 %collective-permute-start.3 = (bf16[320,1024]{1,0:T(8,128)(2,1)}, bf16[320,1024]{1,0:T(8,128)(2,1)S(1)}, u32[]{:S(2)}, u32[]{:S(2)}) collective-permute-start(bf16[320,1024]{1,0:T(8,128)(2,1)} %collective-permute-done.refs_1_), channel_id=1, source_target_pairs={{0,6},{1,7},{2,0},{3,1},{4,2},{5,3},{6,4},{7,5},{8,14},{9,15},{10,... | collective-permute-start | bytes 1966088 | tf_op jit(solution)/shard_map/ppermute | solution.py:46
  48.2 16.4 %collective-permute-start.11 = (bf16[320,1024]{1,0:T(8,128)(2,1)}, bf16[320,1024]{1,0:T(8,128)(2,1)}, u32[]{:S(2)}, u32[]{:S(2)}) collective-permute-start(bf16[320,1024]{1,0:T(8,128)(2,1)} %collective-permute-done.7.refs_9_.refs_2_), channel_id=1, source_target_pairs={{0,32},{1,33},{2,34},{3,35},{4,36},{5,37},{6,38},{7,39},{8,40},{9,... | collective-permute-start | bytes 1966088 | tf_op jit(solution)/shard_map/ppermute | solution.py:46
  50.1 14.5 %collective-permute-start.10 = (bf16[320,1024]{1,0:T(8,128)(2,1)}, bf16[320,1024]{1,0:T(8,128)(2,1)}, u32[]{:S(2)}, u32[]{:S(2)}) collective-permute-start(bf16[320,1024]{1,0:T(8,128)(2,1)} %collective-permute-done.7.refs_9_.refs_2_), channel_id=1, source_target_pairs={{0,96},{1,97},{2,98},{3,99},{4,100},{5,101},{6,102},{7,103},{8,104... | collective-permute-start | bytes 1966088 | tf_op jit(solution)/shard_map/ppermute | solution.py:46
  52.3 0.8 copy-start
  52.3 15.5 %collective-permute-start.8 = (bf16[320,1024]{1,0:T(8,128)(2,1)}, bf16[320,1024]{1,0:T(8,128)(2,1)S(1)}, u32[]{:S(2)}, u32[]{:S(2)}) collective-permute-start(bf16[320,1024]{1,0:T(8,128)(2,1)} %collective-permute-done.2.refs_6_), channel_id=1, source_target_pairs={{0,2},{1,3},{2,4},{3,5},{4,6},{5,7},{6,0},{7,1},{8,10},{9,11},{10,... | collective-permute-start | bytes 1966088 | tf_op jit(solution)/shard_map/ppermute | solution.py:46
  53.1 15.2 %collective-permute-start.9 = (bf16[320,1024]{1,0:T(8,128)(2,1)S(1)}, bf16[320,1024]{1,0:T(8,128)(2,1)S(1)}, u32[]{:S(2)}, u32[]{:S(2)}) collective-permute-start(bf16[320,1024]{1,0:T(8,128)(2,1)S(1)} %collective-permute-done.3.refs_3_), channel_id=1, source_target_pairs={{0,6},{1,7},{2,0},{3,1},{4,2},{5,3},{6,4},{7,5},{8,14},{9,15},{10,... | collective-permute-start | bytes 1966088 | tf_op jit(solution)/shard_map/ppermute | solution.py:46
  64.6 14.7 %collective-permute-start.12 = (bf16[320,1024]{1,0:T(8,128)(2,1)}, bf16[320,1024]{1,0:T(8,128)(2,1)}, u32[]{:S(2)}, u32[]{:S(2)}) collective-permute-start(bf16[320,1024]{1,0:T(8,128)(2,1)} %collective-permute-done.5.refs_14_.refs_7_), channel_id=1, source_target_pairs={{0,32},{1,33},{2,34},{3,35},{4,36},{5,37},{6,38},{7,39},{8,40},{9,... | collective-permute-start | bytes 1966088 | tf_op jit(solution)/shard_map/ppermute | solution.py:46
  65.9 13.4 %collective-permute-start.13 = (bf16[320,1024]{1,0:T(8,128)(2,1)}, bf16[320,1024]{1,0:T(8,128)(2,1)}, u32[]{:S(2)}, u32[]{:S(2)}) collective-permute-start(bf16[320,1024]{1,0:T(8,128)(2,1)} %collective-permute-done.10.refs_11_.refs_4_), channel_id=1, source_target_pairs={{0,96},{1,97},{2,98},{3,99},{4,100},{5,101},{6,102},{7,103},{8,104... | collective-permute-start | bytes 1966088 | tf_op jit(solution)/shard_map/ppermute | solution.py:46
  67.8 12.0 %collective-permute-start.14 = (bf16[320,1024]{1,0:T(8,128)(2,1)}, bf16[320,1024]{1,0:T(8,128)(2,1)}, u32[]{:S(2)}, u32[]{:S(2)}) collective-permute-start(bf16[320,1024]{1,0:T(8,128)(2,1)} %own_text.1.refs_8_.refs_1_), channel_id=1, source_target_pairs={{0,8},{1,9},{2,10},{3,11},{4,12},{5,13},{6,14},{7,15},{8,0},{9,1},... | collective-permute-start | bytes 1966088 | tf_op jit(solution)/shard_map/ppermute | solution.py:46
  67.8 0.8 copy-start.1
  67.8 12.0 %collective-permute-start.15 = (bf16[320,1024]{1,0:T(8,128)(2,1)}, bf16[320,1024]{1,0:T(8,128)(2,1)}, u32[]{:S(2)}, u32[]{:S(2)}) collective-permute-start(bf16[320,1024]{1,0:T(8,128)(2,1)} %collective-permute-done.7.refs_9_.refs_2_), channel_id=1, source_target_pairs={{0,8},{1,9},{2,10},{3,11},{4,12},{5,13},{6,14},{7,15},{8,0},{9,1},... | collective-permute-start | bytes 1966088 | tf_op jit(solution)/shard_map/ppermute | solution.py:46
  68.7 0.8 copy-start.2
  69.5 10.8 %collective-permute-start.16 = (bf16[320,1024]{1,0:T(8,128)(2,1)}, bf16[320,1024]{1,0:T(8,128)(2,1)}, u32[]{:S(2)}, u32[]{:S(2)}) collective-permute-start(bf16[320,1024]{1,0:T(8,128)(2,1)} %collective-permute-done.6.refs_10_.refs_3_), channel_id=1, source_target_pairs={{0,8},{1,9},{2,10},{3,11},{4,12},{5,13},{6,14},{7,15},{8,0},{9,1},... | collective-permute-start | bytes 1966088 | tf_op jit(solution)/shard_map/ppermute | solution.py:46
  79.3 2.6 %collective-permute-start.20 = (bf16[320,1024]{1,0:T(8,128)(2,1)}, bf16[320,1024]{1,0:T(8,128)(2,1)}, u32[]{:S(2)}, u32[]{:S(2)}) collective-permute-start(bf16[320,1024]{1,0:T(8,128)(2,1)} %collective-permute-done.5.refs_14_.refs_7_), channel_id=1, source_target_pairs={{0,8},{1,9},{2,10},{3,11},{4,12},{5,13},{6,14},{7,15},{8,0},{9,1},... | collective-permute-start | bytes 1966088 | tf_op jit(solution)/shard_map/ppermute | solution.py:46
  79.3 3.4 %collective-permute-start.21 = (bf16[320,1024]{1,0:T(8,128)(2,1)}, bf16[320,1024]{1,0:T(8,128)(2,1)}, u32[]{:S(2)}, u32[]{:S(2)}) collective-permute-start(bf16[320,1024]{1,0:T(8,128)(2,1)} %collective-permute-done.11.refs_15_.refs_8_), channel_id=1, source_target_pairs={{0,8},{1,9},{2,10},{3,11},{4,12},{5,13},{6,14},{7,15},{8,0},{9,1},... | collective-permute-start | bytes 1966088 | tf_op jit(solution)/shard_map/ppermute | solution.py:46
  79.8 3.8 %collective-permute-start.17 = (bf16[320,1024]{1,0:T(8,128)(2,1)}, bf16[320,1024]{1,0:T(8,128)(2,1)}, u32[]{:S(2)}, u32[]{:S(2)}) collective-permute-start(bf16[320,1024]{1,0:T(8,128)(2,1)} %collective-permute-done.10.refs_11_.refs_4_), channel_id=1, source_target_pairs={{0,8},{1,9},{2,10},{3,11},{4,12},{5,13},{6,14},{7,15},{8,0},{9,1},... | collective-permute-start | bytes 1966088 | tf_op jit(solution)/shard_map/ppermute | solution.py:46
  79.9 4.6 %collective-permute-start.18 = (bf16[320,1024]{1,0:T(8,128)(2,1)}, bf16[320,1024]{1,0:T(8,128)(2,1)}, u32[]{:S(2)}, u32[]{:S(2)}) collective-permute-start(bf16[320,1024]{1,0:T(8,128)(2,1)} %collective-permute-done.12.refs_12_.refs_5_), channel_id=1, source_target_pairs={{0,8},{1,9},{2,10},{3,11},{4,12},{5,13},{6,14},{7,15},{8,0},{9,1},... | collective-permute-start | bytes 1966088 | tf_op jit(solution)/shard_map/ppermute | solution.py:46
  80.3 5.2 %collective-permute-start.19 = (bf16[320,1024]{1,0:T(8,128)(2,1)}, bf16[320,1024]{1,0:T(8,128)(2,1)}, u32[]{:S(2)}, u32[]{:S(2)}) collective-permute-start(bf16[320,1024]{1,0:T(8,128)(2,1)} %collective-permute-done.13.refs_13_.refs_6_), channel_id=1, source_target_pairs={{0,8},{1,9},{2,10},{3,11},{4,12},{5,13},{6,14},{7,15},{8,0},{9,1},... | collective-permute-start | bytes 1966088 | tf_op jit(solution)/shard_map/ppermute | solution.py:46
  156.8 5.3 %collective-permute-start.24 = (bf16[1280,1024]{1,0:T(8,128)(2,1)}, bf16[1280,1024]{1,0:T(8,128)(2,1)}, u32[]{:S(2)}, u32[]{:S(2)}) collective-permute-start(bf16[1280,1024]{1,0:T(8,128)(2,1)} %get-tuple-element.53), channel_id=1, source_target_pairs={{0,8},{1,9},{2,10},{3,11},{4,12},{5,13},{6,14},{7,15},{8,0},{9,1},... | collective-permute-start | bytes 7864328 | tf_op jit(solution)/shard_map/ppermute | solution.py:46
  156.9 13.0 %collective-permute-start.34 = (bf16[160,1024]{1,0:T(8,128)(2,1)}, bf16[160,1024]{1,0:T(8,128)(2,1)}, u32[]{:S(2)}, u32[]{:S(2)}) collective-permute-start(bf16[160,1024]{1,0:T(8,128)(2,1)} %get-tuple-element.63), channel_id=1, source_target_pairs={{0,2},{1,3},{2,4},{3,5},{4,6},{5,7},{6,0},{7,1},{8,10},{9,11},{10,... | collective-permute-start | bytes 983048 | tf_op jit(solution)/shard_map/ppermute | solution.py:46
  157.5 15.2 %collective-permute-start.35 = (bf16[160,1024]{1,0:T(8,128)(2,1)}, bf16[160,1024]{1,0:T(8,128)(2,1)}, u32[]{:S(2)}, u32[]{:S(2)}) collective-permute-start(bf16[160,1024]{1,0:T(8,128)(2,1)} %get-tuple-element.64), channel_id=1, source_target_pairs={{0,6},{1,7},{2,0},{3,1},{4,2},{5,3},{6,4},{7,5},{8,14},{9,15},{10,... | collective-permute-start | bytes 983048 | tf_op jit(solution)/shard_map/ppermute | solution.py:46
  162.2 6.1 %copy-start.3 = (f32[8,128]{1,0:T(8,128)S(1)}, f32[8,128]{1,0:T(8,128)}, u32[]{:S(2)}) copy-start(f32[8,128]{1,0:T(8,128)} %get-tuple-element.51) | copy-start | bytes 12292
  165.0 12.6 %collective-permute-start.26 = (bf16[160,1024]{1,0:T(8,128)(2,1)}, bf16[160,1024]{1,0:T(8,128)(2,1)}, u32[]{:S(2)}, u32[]{:S(2)}) collective-permute-start(bf16[160,1024]{1,0:T(8,128)(2,1)} %get-tuple-element.55), channel_id=1, source_target_pairs={{0,32},{1,33},{2,34},{3,35},{4,36},{5,37},{6,38},{7,39},{8,40},{9,... | collective-permute-start | bytes 983048 | tf_op jit(solution)/shard_map/ppermute | solution.py:46
  165.0 12.6 %collective-permute-start.27 = (bf16[160,1024]{1,0:T(8,128)(2,1)}, bf16[160,1024]{1,0:T(8,128)(2,1)}, u32[]{:S(2)}, u32[]{:S(2)}) collective-permute-start(bf16[160,1024]{1,0:T(8,128)(2,1)} %get-tuple-element.56), channel_id=1, source_target_pairs={{0,96},{1,97},{2,98},{3,99},{4,100},{5,101},{6,102},{7,103},{8,104... | collective-permute-start | bytes 983048 | tf_op jit(solution)/shard_map/ppermute | solution.py:46
  168.2 1.2 collective-permute-start.22
  169.4 14.0 %collective-permute-start.37 = (bf16[160,1024]{1,0:T(8,128)(2,1)}, bf16[160,1024]{1,0:T(8,128)(2,1)}, u32[]{:S(2)}, u32[]{:S(2)}) collective-permute-start(bf16[160,1024]{1,0:T(8,128)(2,1)} %get-tuple-element.66), channel_id=1, source_target_pairs={{0,2},{1,3},{2,4},{3,5},{4,6},{5,7},{6,0},{7,1},{8,10},{9,11},{10,... | collective-permute-start | bytes 983048 | tf_op jit(solution)/shard_map/ppermute | solution.py:46
  169.9 13.4 %collective-permute-start.23 = (f32[8,128]{1,0:T(8,128)S(1)}, f32[8,128]{1,0:T(8,128)S(1)}, u32[]{:S(2)}, u32[]{:S(2)}) collective-permute-start(f32[8,128]{1,0:T(8,128)S(1)} %add.18), channel_id=1, source_target_pairs={{0,16},{1,17},{2,18},{3,19},{4,20},{5,21},{6,22},{7,23},{8,24},{9,... | collective-permute-start | bytes 12296 | tf_op jit(solution)/shard_map/ppermute | solution.py:53
  174.9 10.4 %collective-permute-start.38 = (bf16[160,1024]{1,0:T(8,128)(2,1)}, bf16[160,1024]{1,0:T(8,128)(2,1)}, u32[]{:S(2)}, u32[]{:S(2)}) collective-permute-start(bf16[160,1024]{1,0:T(8,128)(2,1)} %get-tuple-element.67), channel_id=1, source_target_pairs={{0,6},{1,7},{2,0},{3,1},{4,2},{5,3},{6,4},{7,5},{8,14},{9,15},{10,... | collective-permute-start | bytes 983048 | tf_op jit(solution)/shard_map/ppermute | solution.py:46
  177.6 12.8 %collective-permute-start.29 = (bf16[160,1024]{1,0:T(8,128)(2,1)}, bf16[160,1024]{1,0:T(8,128)(2,1)}, u32[]{:S(2)}, u32[]{:S(2)}) collective-permute-start(bf16[160,1024]{1,0:T(8,128)(2,1)} %get-tuple-element.58), channel_id=1, source_target_pairs={{0,32},{1,33},{2,34},{3,35},{4,36},{5,37},{6,38},{7,39},{8,40},{9,... | collective-permute-start | bytes 983048 | tf_op jit(solution)/shard_map/ppermute | solution.py:46
  180.1 11.7 %collective-permute-start.30 = (bf16[160,1024]{1,0:T(8,128)(2,1)}, bf16[160,1024]{1,0:T(8,128)(2,1)}, u32[]{:S(2)}, u32[]{:S(2)}) collective-permute-start(bf16[160,1024]{1,0:T(8,128)(2,1)} %get-tuple-element.59), channel_id=1, source_target_pairs={{0,96},{1,97},{2,98},{3,99},{4,100},{5,101},{6,102},{7,103},{8,104... | collective-permute-start | bytes 983048 | tf_op jit(solution)/shard_map/ppermute | solution.py:46
  183.3 13.5 %collective-permute-start.25 = (bf16[160,1024]{1,0:T(8,128)(2,1)}, bf16[160,1024]{1,0:T(8,128)(2,1)}, u32[]{:S(2)}, u32[]{:S(2)}) collective-permute-start(bf16[160,1024]{1,0:T(8,128)(2,1)} %get-tuple-element.54), channel_id=1, source_target_pairs={{0,96},{1,97},{2,98},{3,99},{4,100},{5,101},{6,102},{7,103},{8,104... | collective-permute-start | bytes 983048 | tf_op jit(solution)/shard_map/ppermute | solution.py:46
  183.4 14.9 %collective-permute-start.28 = (bf16[160,1024]{1,0:T(8,128)(2,1)}, bf16[160,1024]{1,0:T(8,128)(2,1)}, u32[]{:S(2)}, u32[]{:S(2)}) collective-permute-start(bf16[160,1024]{1,0:T(8,128)(2,1)} %get-tuple-element.57), channel_id=1, source_target_pairs={{0,32},{1,33},{2,34},{3,35},{4,36},{5,37},{6,38},{7,39},{8,40},{9,... | collective-permute-start | bytes 983048 | tf_op jit(solution)/shard_map/ppermute | solution.py:46
  185.3 19.7 %collective-permute-start.33 = (bf16[160,1024]{1,0:T(8,128)(2,1)}, bf16[160,1024]{1,0:T(8,128)(2,1)}, u32[]{:S(2)}, u32[]{:S(2)}) collective-permute-start(bf16[160,1024]{1,0:T(8,128)(2,1)} %get-tuple-element.62), channel_id=1, source_target_pairs={{0,6},{1,7},{2,0},{3,1},{4,2},{5,3},{6,4},{7,5},{8,14},{9,15},{10,... | collective-permute-start | bytes 983048 | tf_op jit(solution)/shard_map/ppermute | solution.py:46
  190.4 14.6 %collective-permute-start.36 = (bf16[160,1024]{1,0:T(8,128)(2,1)}, bf16[160,1024]{1,0:T(8,128)(2,1)}, u32[]{:S(2)}, u32[]{:S(2)}) collective-permute-start(bf16[160,1024]{1,0:T(8,128)(2,1)} %get-tuple-element.65), channel_id=1, source_target_pairs={{0,2},{1,3},{2,4},{3,5},{4,6},{5,7},{6,0},{7,1},{8,10},{9,11},{10,... | collective-permute-start | bytes 983048 | tf_op jit(solution)/shard_map/ppermute | solution.py:46
  191.8 13.2 %collective-permute-start.39 = (bf16[160,1024]{1,0:T(8,128)(2,1)}, bf16[160,1024]{1,0:T(8,128)(2,1)}, u32[]{:S(2)}, u32[]{:S(2)}) collective-permute-start(bf16[160,1024]{1,0:T(8,128)(2,1)} %pair_sum.2), channel_id=1, source_target_pairs={{0,1},{1,0},{2,3},{3,2},{4,5},{5,4},{6,7},{7,6},{8,9},{9,8},{10,11... | collective-permute-start | bytes 983048 | tf_op jit(solution)/shard_map/ppermute | solution.py:46
  196.8 11.9 %collective-permute-start.40 = (bf16[160,1024]{1,0:T(8,128)(2,1)}, bf16[160,1024]{1,0:T(8,128)(2,1)}, u32[]{:S(2)}, u32[]{:S(2)}) collective-permute-start(bf16[160,1024]{1,0:T(8,128)(2,1)} %pair_sum.3), channel_id=1, source_target_pairs={{0,16},{1,17},{2,18},{3,19},{4,20},{5,21},{6,22},{7,23},{8,24},{9,... | collective-permute-start | bytes 983048 | tf_op jit(solution)/shard_map/ppermute | solution.py:46
  198.2 3.6 %collective-permute-start.31 = (f32[8,128]{1,0:T(8,128)S(1)}, f32[8,128]{1,0:T(8,128)S(1)}, u32[]{:S(2)}, u32[]{:S(2)}) collective-permute-start(f32[8,128]{1,0:T(8,128)S(1)} %add.19), channel_id=1, source_target_pairs={{0,32},{1,33},{2,34},{3,35},{4,36},{5,37},{6,38},{7,39},{8,40},{9,... | collective-permute-start | bytes 12296 | tf_op jit(solution)/shard_map/ppermute | solution.py:53
  201.8 5.7 %collective-permute-start.32 = (f32[8,128]{1,0:T(8,128)S(1)}, f32[8,128]{1,0:T(8,128)S(1)}, u32[]{:S(2)}, u32[]{:S(2)}) collective-permute-start(f32[8,128]{1,0:T(8,128)S(1)} %add.20), channel_id=1, source_target_pairs={{0,64},{1,65},{2,66},{3,67},{4,68},{5,69},{6,70},{7,71},{8,72},{9,... | collective-permute-start | bytes 12296 | tf_op jit(solution)/shard_map/ppermute | solution.py:53
